TPU v7x, 128 devices: a whole 4x4x4 slice. The times are simulated.
128 devices in a mesh: dp: 32 (over z, y, core), hid: 4 (over x).
Axes of the slice: x: 4, y: 4, z: 4, core: 2. Of those that a mesh axis runs over, the one named last changes fastest.
Arguments:
- gate_pre: bfloat16 [4096, 2, 8192], P('dp', None, 'hid'), may hold values from -6 to 6
- up_pre: bfloat16 [4096, 2, 8192], P('dp', None, 'hid'), may hold values from -6 to 6
- out_grad: bfloat16 [4096, 6144], P('dp'), may hold values from -6 to 6
- combine: float32 [4096, 2], P('dp'), may hold values from 0.1 to 0.9
- expert_ids: int32 [4096, 2], P('dp'), may hold values from 0 to 7, all different within a row; in each aligned block of 128 rows (0 to 127, 128 to 255, ...) at most 48 rows name the same one
- down_weight: bfloat16 [32, 8192, 1536], P('dp', 'hid'), may hold values from -0.0625 to 0.0625
Outputs:
- mixed: bfloat16 [4096, 4, 1536], P('dp', None, 'hid')
- combine_grad: float32 [4096, 2], P('dp')
- gate_grad: bfloat16 [4096, 2, 8192], P('dp', None, 'hid')
- up_grad: bfloat16 [4096, 2, 8192], P('dp', None, 'hid')
- weight_grad: bfloat16 [32, 8192, 1536], P('dp', 'hid')
Inputs may be any that keep to these rules, and one draw needn't show every extreme that they name: `expert_ids`: each token names two different experts. Among the 128 tokens of one dp index no expert is named by more than 48 tokens, and in every draw some expert is named by exactly 48 of them.
All inputs are finite; a program needn't handle non-finite values.
Results may differ from a plain program's by a relative error of at most 0.0057.
Values may be sent and summed in bfloat16 or wider, within the bound.
A program may use at most 448 MiB of HBM per device.

v0:
```python
import jax
import jax.numpy as jnp
from jax import lax
from jax.sharding import PartitionSpec as P

E = 8
TOP = 2
CAP = 48


def per_device(gate_pre, up_pre, out_grad, combine, expert_ids, down_weight):
    dp_count = lax.axis_size("dp")
    hid_count = lax.axis_size("hid")
    experts = E
    slices = dp_count // experts
    capacity = CAP
    tokens_here = gate_pre.shape[0]
    local_ff = gate_pre.shape[2]
    slice_width = down_weight.shape[2]
    quarter = slice_width // hid_count
    slot_count = tokens_here * TOP
    flat_ids = expert_ids.reshape(slot_count)
    onehot = (flat_ids[:, None] == jnp.arange(experts, dtype=jnp.int32)[None, :]).astype(jnp.int32)
    earlier = jnp.cumsum(onehot, axis=0) - onehot
    position = jnp.sum(earlier * onehot, axis=1)
    target = flat_ids * capacity + position
    routing_table = (
        target[None, :] == jnp.arange(experts * capacity, dtype=jnp.int32)[:, None]
    ).astype(jnp.int32)
    slot_numbers = jnp.arange(slot_count, dtype=jnp.int32)
    filled = jnp.sum(routing_table, axis=1)
    source_slot = jnp.sum(routing_table * slot_numbers[None, :], axis=1) + (1 - filled) * (
        slot_count * slices
    )
    source_slot = source_slot.reshape(experts, 1, capacity)
    slice_index = jnp.arange(slices, dtype=jnp.int32).reshape(1, slices, 1)
    gate_f = gate_pre.astype(jnp.float32)
    up_f = up_pre.astype(jnp.float32)
    sigmoid_gate = jax.nn.sigmoid(gate_f)
    hidden = (gate_f * sigmoid_gate * up_f).astype(jnp.bfloat16).reshape(slot_count, local_ff)
    scaled = (combine[:, :, None] * out_grad[:, None, :].astype(jnp.float32)).astype(jnp.bfloat16)
    scaled_rows = scaled.reshape(slot_count * slices, slice_width)
    hidden_index = jnp.broadcast_to(source_slot, (experts, slices, capacity)).reshape(
        dp_count * capacity
    )
    grad_index = (source_slot * slices + slice_index).reshape(dp_count * capacity)
    send_hidden = jnp.take(hidden, hidden_index, axis=0, mode="fill", fill_value=0).reshape(
        dp_count, capacity, local_ff
    )
    send_grad = jnp.take(scaled_rows, grad_index, axis=0, mode="fill", fill_value=0).reshape(
        dp_count, capacity, slice_width
    )
    got_hidden, got_grad = (
        lax.all_to_all(send_hidden, "dp", split_axis=0, concat_axis=0, tiled=True),
        lax.all_to_all(send_grad, "dp", split_axis=0, concat_axis=0, tiled=True),
    )
    hidden_rows = got_hidden.reshape(dp_count * capacity, local_ff)
    grad_rows = got_grad.reshape(dp_count * capacity, slice_width)
    weights = down_weight[0]
    expert_out = jnp.dot(hidden_rows, weights, preferred_element_type=jnp.float32)
    partial_back = lax.dot_general(
        grad_rows, weights, (((1,), (1,)), ((), ())), preferred_element_type=jnp.float32
    )
    weight_grad = lax.dot_general(
        hidden_rows, grad_rows, (((0,), (0,)), ((), ())), preferred_element_type=jnp.float32
    )
    weight_grad = weight_grad.astype(jnp.bfloat16)[None]
    partial_back = partial_back.reshape(dp_count, capacity, local_ff)
    return_index = (
        (flat_ids[:, None] * slices + jnp.arange(slices, dtype=jnp.int32)[None, :]) * capacity
        + position[:, None]
    ).reshape(slot_count * slices)
    back_out, back_grad = (
        lax.all_to_all(
            expert_out.reshape(dp_count, capacity, slice_width),
            "dp",
            split_axis=0,
            concat_axis=0,
            tiled=True,
        ),
        lax.all_to_all(partial_back, "dp", split_axis=0, concat_axis=0, tiled=True),
    )
    slot_part = jnp.take(back_out.reshape(dp_count * capacity, slice_width), return_index, axis=0)
    slot_part = slot_part.reshape(slot_count, slices, slice_width)
    slot_out = lax.psum_scatter(slot_part, "hid", scatter_dimension=2, tiled=True)
    grad_parts = jnp.take(back_grad.reshape(dp_count * capacity, local_ff), return_index, axis=0)
    hidden_grad = jnp.sum(grad_parts.reshape(slot_count, slices, local_ff), axis=1)
    slot_out = slot_out.reshape(tokens_here, TOP, slices, quarter)
    mixed = jnp.sum(combine[:, :, None, None] * slot_out, axis=1).astype(jnp.bfloat16)
    hid_index = lax.axis_index("hid")
    grad_view = out_grad.reshape(tokens_here, slices, hid_count, quarter)
    my_columns = lax.dynamic_index_in_dim(grad_view, hid_index, 2, keepdims=False).astype(
        jnp.float32
    )
    local_terms = jnp.sum(my_columns[:, None] * slot_out, axis=(2, 3))
    combine_grad = lax.psum(local_terms, "hid")
    hidden_grad = hidden_grad.reshape(tokens_here, TOP, local_ff)
    gate_grad = (hidden_grad * up_f * sigmoid_gate * (1.0 + gate_f * (1.0 - sigmoid_gate))).astype(
        jnp.bfloat16
    )
    up_grad = (hidden_grad * gate_f * sigmoid_gate).astype(jnp.bfloat16)
    return (mixed, combine_grad, gate_grad, up_grad, weight_grad)


def solution(mesh):
    return jax.shard_map(
        per_device,
        mesh=mesh,
        in_specs=(
            P("dp", None, "hid"),
            P("dp", None, "hid"),
            P("dp", None),
            P("dp", None),
            P("dp", None),
            P("dp", "hid", None),
        ),
        out_specs=(
            P("dp", None, "hid"),
            P("dp", None),
            P("dp", None, "hid"),
            P("dp", None, "hid"),
            P("dp", "hid", None),
        ),
        check_vma=False,
    )
```

profile of v0, /device:TPU:1, one launch (start us, length us, event | category | flops | bytes accessed | tf_op | source)
XLA Modules:
  0.0 994.6 jit_solution(3746411224963578319)
XLA Ops:
  7.2 0.8 copy.24
  8.0 0.1 broadcast_in_dim_reshape.4
  8.1 0.1 eq.39
  8.2 0.8 copy.23
  9.0 0.6 reduce-window.6
  9.6 0.2 slice_reduce_fusion
  9.9 0.1 fusion.17
  10.0 0.2 convert_reduce_fusion
  10.2 0.1 add.191
  10.3 0.1 add.207
  10.5 1.7 convert_element_type.61
  12.2 0.0 copy-done.6
  12.2 4.1 multiply_convert_fusion
  16.3 6.9 convert_element_type.63
  23.2 6.2 gather_fusion.2
  29.4 2.7 broadcast_select_fusion.1
  32.2 65.9 %all_to_all.20 = bf16[32,48,1536]{2,1,0:T(8,128)(2,1)S(1)} all-to-all(bf16[32,48,1536]{2,1,0:T(8,128)(2,1)S(1)} %broadcast_select_fusion.1), channel_id=1, replica_groups=mesh['dp'=32,'hid'=4] {'dp'}, dimensions={0} | all-to-all | bytes 9437184 | tf_op jit(solution)/shard_map/all_to_all | solution.py:55
  98.1 2.1 copy-done.2
  100.2 14.7 %fusion.1 = f32[32,48,2048]{2,1,0:T(8,128)} fusion(bf16[32,48,1536]{2,1,0:T(8,128)(2,1)S(1)} %all_to_all.20, bf16[1,2048,1536]{2,1,0:T(8,128)(2,1)} %param.11), kind=kOutput, calls=%fused_computation.7 | convolution fusion | flops 9663676416 | bytes 23592960 | tf_op jit(solution)/shard_map/dot_general | solution.py:61
  114.9 5.1 all-to-all-start.3
  120.0 0.0 reduce-scatter.4.cloned.1.call-start
  120.1 0.1 reshape.282
  120.1 0.1 multiply_add_fusion
  120.3 0.1 add.197
  120.5 0.1 compare_and_fusion
  120.6 150.8 %all-to-all-done.3 = f32[32,48,2048]{2,1,0:T(8,128)} async-done(((f32[32,48,2048]{2,1,0:T(8,128)}), f32[32,48,2048]{2,1,0:T(8,128)}, u32[]{:S(2)}, u32[]{:S(2)}) %all-to-all-start.3) | async-done | bytes 12582944 | tf_op jit(solution)/shard_map/all_to_all | solution.py:81
  271.5 13.8 %gather_fusion.3 = f32[1024,2048]{1,0:T(8,128)} fusion(f32[1536,2048]{1,0:T(8,128)} %bitcast.12, s32[1024]{0:T(1024)S(1)} %broadcast_clamp_fusion), kind=kCustom, calls=%fused_computation.3 | custom fusion | bytes 16781312 | tf_op jit(solution)/shard_map/jit(_take)/gather | solution.py:86
  285.3 9.8 gather.31
  295.0 11.5 %select_reduce_fusion = f32[256,2048]{1,0:T(8,128)} fusion(f32[256,4,2048]{2,1,0:T(4,128)} %gather.31, pred[256,4]{1,0:T(8,128)(4,1)S(1)} %compare_and_fusion), kind=kLoop, calls=%fused_computation.5 | loop fusion | flops 3670016 | bytes 10486784 | tf_op jit(solution)/shard_map/reduce_sum | solution.py:87
  306.5 2.6 reshape.287
  309.1 0.0 copy-done.3
  309.1 0.0 copy-start.4
  309.1 0.0 copy-start.5
  309.1 3.1 fusion.14
  312.2 0.0 copy-done.4
  312.2 0.0 copy-done.5
  312.2 4.1 fusion.8
  316.3 0.8 reshape.281
  317.2 7.0 gather_fusion
  324.1 3.3 broadcast_select_fusion
  327.4 85.9 %all_to_all.21 = bf16[32,48,2048]{2,1,0:T(8,128)(2,1)S(1)} all-to-all(bf16[32,48,2048]{2,1,0:T(8,128)(2,1)S(1)} %broadcast_select_fusion), channel_id=1, replica_groups=mesh['dp'=32,'hid'=4] {'dp'}, dimensions={0} | all-to-all | bytes 12582912 | tf_op jit(solution)/shard_map/all_to_all | solution.py:54
  413.3 14.5 %fusion.3 = f32[32,48,1536]{2,1,0:T(8,128)S(1)} fusion(bf16[32,48,2048]{2,1,0:T(8,128)(2,1)S(1)} %all_to_all.21, bf16[1,2048,1536]{2,1,0:T(8,128)(2,1)} %param.11), kind=kOutput, calls=%fused_computation.9 | convolution fusion | flops 9663676416 | bytes 22020096 | tf_op jit(solution)/shard_map/dot_general | solution.py:60
  427.9 0.0 copy-done
  427.9 112.3 %all_to_all.22 = f32[32,48,1536]{2,1,0:T(8,128)} all-to-all(f32[32,48,1536]{2,1,0:T(8,128)S(1)} %fusion.3), channel_id=1, replica_groups=mesh['dp'=32,'hid'=4] {'dp'}, dimensions={0} | all-to-all | bytes 18874368 | tf_op jit(solution)/shard_map/all_to_all | solution.py:74
  540.2 11.3 %gather_fusion.1 = f32[1024,1536]{1,0:T(8,128)} fusion(f32[1536,1536]{1,0:T(8,128)} %bitcast.42, s32[1024]{0:T(1024)S(1)} %broadcast_clamp_fusion), kind=kCustom, calls=%fused_computation.1 | custom fusion | bytes 12587008 | tf_op jit(solution)/shard_map/jit(_take)/gather | solution.py:83
  551.5 7.6 gather.27
  559.1 7.0 broadcast_select_fusion.2
  566.1 95.9 %copy.28 = f32[256,4,1536]{1,0,2:T(8,128)} copy(f32[256,4,1536]{2,1,0:T(4,128)} %broadcast_select_fusion.2) | data formatting | bytes 12582912
  662.0 164.7 %reshape.323 = f32[1536,1024]{1,0:T(8,128)} reshape(f32[1536,256,4]{2,1,0:T(8,128)} %bitcast.15) | data formatting | bytes 12582912
  826.7 0.0 reduce-scatter.4.cloned.1.call-update
  826.7 1.4 copy-done.1
  828.1 1.2 reshape.285
  829.3 0.7 dynamic-slice_convert_fusion
  830.0 0.2 copy.32
  830.2 15.2 %fusion = bf16[1,2048,1536]{2,1,0:T(8,128)(2,1)} fusion(bf16[32,48,2048]{2,1,0:T(8,128)(2,1)} %copy-done, bf16[32,48,1536]{2,1,0:T(8,128)(2,1)} %copy-done.2), kind=kOutput, calls=%fused_computation.6 | convolution fusion | flops 9666822144 | bytes 17301504 | tf_op jit(solution)/shard_map/dot_general | solution.py:64
  845.5 43.9 %reduce-scatter.4.cloned.1.call-done = f32[384,1024]{1,0:T(8,128)} async-done(((f32[1536,1024]{1,0:T(8,128)}), f32[384,1024]{1,0:T(8,128)}) %reduce-scatter.4.cloned.1.call-update) | async-done | bytes 1572880
  889.4 54.3 %reshape.324 = f32[384,256,4]{2,1,0:T(8,128)} reshape(f32[384,1024]{1,0:T(8,128)} %reduce-scatter.4.cloned.1.call-done) | data formatting | bytes 3145728
  943.7 28.3 %copy.29 = f32[256,4,384]{2,1,0:T(4,128)S(1)} copy(f32[256,4,384]{1,0,2:T(8,128)} %bitcast.43) | data formatting | bytes 3145728
  972.0 0.0 copy-done.7
  972.0 1.5 multiply_reduce_fusion
  973.5 1.0 fusion.15
  974.5 0.1 reduce_sum.61
  974.6 12.2 %psum.7 = f32[128,2]{1,0:T(8,128)S(1)} all-reduce(f32[128,2]{1,0:T(8,128)S(1)} %reduce_sum.61), channel_id=1, replica_groups=mesh['dp'=32,'hid'=4] {'hid'}, use_global_device_ids=true, to_apply=%region_8.9 | all-reduce | flops 256 | bytes 2048 | tf_op jit(solution)/shard_map/psum | solution.py:96
  986.9 0.6 copy.27
  (22 shorter events, 0.2 us)
Async XLA Ops:
  9.0 3.2 copy-start.6
  98.1 2.2 copy-start.2
  114.9 156.6 %all-to-all-start.3 = ((f32[32,48,2048]{2,1,0:T(8,128)}), f32[32,48,2048]{2,1,0:T(8,128)}, u32[]{:S(2)}, u32[]{:S(2)}) async-start(f32[32,48,2048]{2,1,0:T(8,128)} %fusion.1), calls=%async_computation.3 | async-start | bytes 25165824 | tf_op jit(solution)/shard_map/all_to_all | solution.py:81
  120.0 769.4 %reduce-scatter.4.cloned.1.call-start = ((), (), s32[]{:S(2)}) async-start(), calls=%async_computation.5 | async-start | bytes 7864320
  306.5 2.6 copy-start.3
  309.1 3.1 copy-start.4
  309.1 3.1 copy-start.5
  413.3 14.5 %copy-start = (bf16[32,48,2048]{2,1,0:T(8,128)(2,1)}, bf16[32,48,2048]{2,1,0:T(8,128)(2,1)S(1)}, u32[]{:S(2)}) copy-start(bf16[32,48,2048]{2,1,0:T(8,128)(2,1)S(1)} %all_to_all.21) | copy-start | bytes 18874372
  826.7 1.4 copy-start.1
  943.7 28.3 %copy-start.7 = (f32[128,2]{1,0:T(8,128)S(1)}, f32[128,2]{1,0:T(8,128)}, u32[]{:S(2)}) copy-start(f32[128,2]{1,0:T(8,128)} %copy-done.6) | copy-start | bytes 3076
Sparse Core Ops, SparseCore 0:
  826.9 62.4 reduce-scatter.3
where the time goes:
time: 1010 us; the launch traced here: 995 us
  local copies, waits for them, and re-layouts  417 us (41%)
  blocking collectives  276 us (27%)
  waiting for transfers between devices  195 us (19%)
  matrix products  44.5 us (4%)
  other arithmetic  42 us (4%)
  between operations  14.6 us (1%)
    unnamed x24, local copies, waits for them, and re-layouts  349 us
    all_to_all x1, waiting for transfers between devices, per_device(): lax.all_to_all(partial_back, 'dp', split_axis=0, concat_axis=0, tiled=True)  151 us
    all_to_all x1, blocking collectives, per_device(): lax.all_to_all(expert_out.reshape(dp_count, capacity, slice_width), 'dp',...  112 us
    all_to_all x1, blocking collectives, per_device(): lax.all_to_all(send_hidden, 'dp', split_axis=0, concat_axis=0, tiled=True)  85.9 us
    all_to_all x1, blocking collectives, per_device(): lax.all_to_all(send_grad, 'dp', split_axis=0, concat_axis=0, tiled=True)  65.9 us
    unnamed x2, waiting for transfers between devices  43.9 us
    gather x2, local copies, waits for them, and re-layouts, per_device(): jnp.take(back_grad.reshape(dp_count * capacity, local_ff), return_index,...  23.6 us
  transfers between devices with their start and end apart: 2, of which 2 were waited for; matrix products, arithmetic and copies ran while one was open for 2% of the time, Pallas kernels for 0%

commit v1 on v0

v1 whole, which is shorter than its diff:
```python
import jax
import jax.numpy as jnp
from jax import lax
from jax.experimental import pallas as pl
from jax.experimental.pallas import tpu as pltpu
from jax.sharding import PartitionSpec as P

E = 8
TOP = 2
CAP = 48
F32 = jnp.float32
BF16 = jnp.bfloat16
MESH = pl.DeviceIdType.MESH


def exchange_kernel(
    hs, gs, w, oh, bh, wg, cg,
    hr, gr, os, orx, od, bs, br, wt, cgs, cgr,
    send_h, send_g, recv_h, recv_g, xg_send, xg_recv, sib_send, sib_recv,
    xo_send, xo_recv, bsib_send, bsib_recv, home_o_send, home_b_send,
    home_recv, wg_sem, cg_send, cg_recv,
):
    me = lax.axis_index("dp")
    x = lax.axis_index("hid")
    z = lax.div(me, 8)
    yc = lax.rem(me, 8)
    core = lax.rem(me, 2)
    e_me = lax.div(me, 4)
    j_me = lax.rem(me, 4)
    sibling = me + 1 - 2 * core
    rows_n = 8 * CAP
    q_w = gr.shape[1] // 4
    half_w = hr.shape[1] // 2

    def m(v, k):
        return pl.multiple_of(v, k)

    barrier = pltpu.get_barrier_semaphore()

    def greet_dp(n, carry):
        peer = lax.rem(me + n, 32)
        pl.semaphore_signal(barrier, inc=1, device_id=(peer, x), device_id_type=MESH)
        return carry

    lax.fori_loop(1, 32, greet_dp, 0)
    for o in range(1, 4):
        pl.semaphore_signal(
            barrier, inc=1, device_id=(me, lax.rem(x + o, 4)), device_id_type=MESH
        )
    pl.semaphore_wait(barrier, 34)

    my_half = m(core * half_w, 128)
    other_half = m((1 - core) * half_w, 128)
    my_quarter = m(x * q_w, 128)
    my_rows = m(me * CAP, 16)
    my_expert_rows = m(e_me * CAP, 16)

    def base_of(r):
        return m(lax.rem(z - r + 4, 4) * rows_n, 16)

    def partner(n):
        return lax.rem(z + lax.div(n, 8), 4) * 8 + lax.rem(yc + lax.rem(n, 8), 8)

    pltpu.make_async_copy(
        gs.at[pl.ds(my_expert_rows, CAP), pl.ds(m(j_me * q_w, 128), q_w)],
        gr.at[pl.ds(my_rows, CAP), pl.ds(my_quarter, q_w)],
        recv_g.at[0],
    ).start()
    pltpu.make_async_copy(
        hs.at[pl.ds(my_expert_rows, CAP), pl.ds(my_half, half_w)],
        hr.at[pl.ds(my_rows, CAP), pl.ds(my_half, half_w)],
        recv_h.at[0],
    ).start()

    def g_copy(n):
        p = partner(n)
        return pltpu.make_async_remote_copy(
            src_ref=gs.at[
                pl.ds(m(lax.div(p, 4) * CAP, 16), CAP), pl.ds(m(lax.rem(p, 4) * q_w, 128), q_w)
            ],
            dst_ref=gr.at[pl.ds(my_rows, CAP), pl.ds(my_quarter, q_w)],
            send_sem=send_g.at[n],
            recv_sem=recv_g.at[lax.div(n, 8)],
            device_id=(p, x),
            device_id_type=MESH,
        )

    def h_copy(n):
        p = partner(n)
        cols = pl.ds(m(lax.rem(p, 2) * half_w, 128), half_w)
        return pltpu.make_async_remote_copy(
            src_ref=hs.at[pl.ds(m(lax.div(p, 4) * CAP, 16), CAP), cols],
            dst_ref=hr.at[pl.ds(my_rows, CAP), cols],
            send_sem=send_h.at[n],
            recv_sem=recv_h.at[lax.div(n, 8)],
            device_id=(p, x),
            device_id_type=MESH,
        )

    def loop(lo, hi, f):
        def step(n, carry):
            f(n)
            return carry

        lax.fori_loop(lo, hi, step, 0)

    loop(1, 32, lambda n: g_copy(n).start())
    loop(1, 32, lambda n: h_copy(n).start())

    def xg_copy(r, o):
        part = gr.at[pl.ds(base_of(r), rows_n), pl.ds(my_quarter, q_w)]
        return pltpu.make_async_remote_copy(
            src_ref=part, dst_ref=part,
            send_sem=xg_send.at[r, o - 1], recv_sem=xg_recv.at[r, o - 1],
            device_id=(me, lax.rem(x + o, 4)), device_id_type=MESH,
        )

    def xg_wait(r, o):
        cols = m(lax.rem(x - o + 4, 4) * q_w, 128)
        part = gr.at[pl.ds(base_of(r), rows_n), pl.ds(cols, q_w)]
        pltpu.make_async_copy(part, part, xg_recv.at[r, o - 1]).wait()

    def pass_g(r):
        part = gr.at[pl.ds(base_of(r), rows_n), pl.ds(my_quarter, q_w)]
        pltpu.make_async_copy(part, part, recv_g.at[r]).wait()
        for o in range(1, 4):
            xg_copy(r, o).start()

    loop(0, 4, pass_g)

    def sib_copy(r):
        part = hr.at[pl.ds(base_of(r), rows_n), pl.ds(my_half, half_w)]
        return pltpu.make_async_remote_copy(
            src_ref=part, dst_ref=part, send_sem=sib_send.at[r], recv_sem=sib_recv.at[r],
            device_id=(sibling, x), device_id_type=MESH,
        )

    def pass_h(r):
        part = hr.at[pl.ds(base_of(r), rows_n), pl.ds(my_half, half_w)]
        pltpu.make_async_copy(part, part, recv_h.at[r]).wait()
        sib_copy(r).start()

    def xo_copy(r, o):
        peer = lax.rem(x + o, 4)
        return pltpu.make_async_remote_copy(
            src_ref=os.at[pl.ds(base_of(r), rows_n), pl.ds(m(peer * q_w, 128), q_w)],
            dst_ref=orx.at[o - 1, pl.ds(base_of(r), rows_n), :],
            send_sem=xo_send.at[r, o - 1], recv_sem=xo_recv.at[r, o - 1],
            device_id=(me, peer), device_id_type=MESH,
        )

    def out_product(r):
        part = hr.at[pl.ds(base_of(r), rows_n), pl.ds(other_half, half_w)]
        pltpu.make_async_copy(part, part, sib_recv.at[r]).wait()
        rows = pl.ds(base_of(r), rows_n)

        def tile(q):
            cols = pl.ds(m(q * 2 * q_w, 128), 2 * q_w)
            acc = jnp.dot(hr[rows, :], w[:, cols], preferred_element_type=F32)
            os[rows, cols] = acc.astype(BF16)

        loop(0, 2, tile)
        for o in range(1, 4):
            xo_copy(r, o).start()

    pass_h(0)

    def h_step(r):
        pass_h(r + 1)
        out_product(r)

    loop(0, 3, h_step)
    out_product(3)

    def bsib_copy(r):
        rows = pl.ds(base_of(r), rows_n)
        return pltpu.make_async_remote_copy(
            src_ref=bs.at[rows, pl.ds(other_half, half_w)],
            dst_ref=br.at[rows, :],
            send_sem=bsib_send.at[r], recv_sem=bsib_recv.at[r],
            device_id=(sibling, x), device_id_type=MESH,
        )

    def back_product(r):
        for o in range(1, 4):
            xg_wait(r, o)
        rows = pl.ds(base_of(r), rows_n)

        def tile(n):
            cols = pl.ds(m(n * 512, 128), 512)
            acc = lax.dot_general(
                gr[rows, :], w[cols, :], (((1,), (1,)), ((), ())), preferred_element_type=F32
            )
            bs[rows, cols] = acc.astype(BF16)

        loop(0, 4, tile)
        bsib_copy(r).start()

    def home_b_copy(n):
        p = lax.rem(z - lax.div(n, 8) + 4, 4) * 8 + lax.rem(yc + lax.rem(n, 8), 8)
        return pltpu.make_async_remote_copy(
            src_ref=br.at[pl.ds(m(p * CAP, 16), CAP), :],
            dst_ref=bh.at[
                pl.ds(m((lax.div(j_me, 2) * E + e_me) * CAP, 16), CAP), pl.ds(my_half, half_w)
            ],
            send_sem=home_b_send.at[n], recv_sem=home_recv.at[1],
            device_id=(p, x), device_id_type=MESH,
        )

    def home_o_copy(n):
        p = lax.rem(z - lax.div(n, 8) + 4, 4) * 8 + lax.rem(yc + lax.rem(n, 8), 8)
        return pltpu.make_async_remote_copy(
            src_ref=od.at[pl.ds(m(p * CAP, 16), CAP), :],
            dst_ref=oh.at[pl.ds(my_expert_rows, CAP), pl.ds(m(j_me * q_w, 128), q_w)],
            send_sem=home_o_send.at[n], recv_sem=home_recv.at[0],
            device_id=(p, x), device_id_type=MESH,
        )

    def back_sum(r):
        rows = pl.ds(base_of(r), rows_n)
        part = br.at[rows, :]
        pltpu.make_async_copy(part, part, bsib_recv.at[r]).wait()

        def tile(i):
            sub = pl.ds(m(base_of(r) + i * CAP, 16), CAP)
            total = br[sub, :].astype(F32) + bs[sub, pl.ds(my_half, half_w)].astype(F32)
            br[sub, :] = total.astype(BF16)

        loop(0, 8, tile)

    def out_sum(r):
        for o in range(1, 4):
            part = orx.at[o - 1, pl.ds(base_of(r), rows_n), :]
            pltpu.make_async_copy(part, part, xo_recv.at[r, o - 1]).wait()

        def tile(i):
            sub = pl.ds(m(base_of(r) + i * CAP, 16), CAP)
            total = os[sub, pl.ds(my_quarter, q_w)].astype(F32)
            for k in range(3):
                total = total + orx[k, sub, :].astype(F32)
            od[sub, :] = total.astype(BF16)

        loop(0, 8, tile)

    def back_first():
        back_sum(0)
        pltpu.make_async_copy(
            br.at[pl.ds(my_rows, CAP), :],
            bh.at[
                pl.ds(m((lax.div(j_me, 2) * E + e_me) * CAP, 16), CAP), pl.ds(my_half, half_w)
            ],
            home_recv.at[1],
        ).start()
        loop(1, 8, lambda n: home_b_copy(n).start())

    def back_next(r):
        back_sum(r)
        loop(r * 8, r * 8 + 8, lambda n: home_b_copy(n).start())

    back_product(0)
    back_product(1)
    back_first()

    def b_step(r):
        back_product(r + 1)
        back_next(r)

    loop(1, 3, b_step)
    back_next(3)

    def wg_copy(n):
        rows = pl.ds(m(n * 256, 16), 256)
        return pltpu.make_async_copy(wt.at[rows, :], wg.at[rows, :], wg_sem.at[n])

    def wg_tile(n):
        cols = pl.ds(m(n * 256, 128), 256)
        acc = lax.dot_general(
            hr[:, cols], gr[...], (((0,), (0,)), ((), ())), preferred_element_type=F32
        )
        wt[pl.ds(m(n * 256, 16), 256), :] = acc.astype(BF16)
        wg_copy(n).start()

    def out_first():
        out_sum(0)
        pltpu.make_async_copy(
            od.at[pl.ds(my_rows, CAP), :],
            oh.at[pl.ds(my_expert_rows, CAP), pl.ds(m(j_me * q_w, 128), q_w)],
            home_recv.at[0],
        ).start()
        loop(1, 8, lambda n: home_o_copy(n).start())

    def out_next(r):
        out_sum(r)
        loop(r * 8, r * 8 + 8, lambda n: home_o_copy(n).start())

    loop(0, 8, wg_tile)
    out_first()
    loop(1, 4, out_next)

    pltpu.make_async_copy(oh, oh, home_recv.at[0]).wait()
    fold = jnp.zeros((rows_n, 128), F32)
    for k in range(4 * q_w // 128):
        cols = slice(k * 128, (k + 1) * 128)
        fold = fold + oh[:, cols].astype(F32) * gs[:, cols].astype(F32)
    high = fold.astype(BF16)
    low = (fold - high.astype(F32)).astype(BF16)
    ones = jnp.ones((8, 128), BF16)
    last = (((1,), (1,)), ((), ()))
    cgs[...] = lax.dot_general(ones, high, last, preferred_element_type=F32) + lax.dot_general(
        ones, low, last, preferred_element_type=F32
    )

    def cg_copy(o):
        return pltpu.make_async_remote_copy(
            src_ref=cgs, dst_ref=cgr.at[o - 1],
            send_sem=cg_send.at[o - 1], recv_sem=cg_recv.at[o - 1],
            device_id=(me, lax.rem(x + o, 4)), device_id_type=MESH,
        )

    for o in range(1, 4):
        cg_copy(o).start()
    for o in range(1, 4):
        cg_copy(o).wait_recv()
    cg[...] = cgs[...] + cgr[0] + cgr[1] + cgr[2]

    pltpu.make_async_copy(bh, bh, home_recv.at[1]).wait()
    for o in range(1, 4):
        cg_copy(o).wait_send()
    loop(0, 8, lambda n: wg_copy(n).wait())

    def drain(n):
        g_copy(n).wait_send()
        h_copy(n).wait_send()
        home_b_copy(n).wait_send()
        home_o_copy(n).wait_send()

    loop(1, 32, drain)

    def drain_r(r):
        sib_copy(r).wait_send()
        bsib_copy(r).wait_send()
        for o in range(1, 4):
            xg_copy(r, o).wait_send()
            xo_copy(r, o).wait_send()

    loop(0, 4, drain_r)


def exchange(hs, gs, w):
    rows, ff = hs.shape
    width = gs.shape[1]
    rows_all = 32 * CAP
    vmem = pl.BlockSpec(memory_space=pltpu.VMEM)
    dma = pltpu.SemaphoreType.DMA
    return pl.pallas_call(
        exchange_kernel,
        out_shape=(
            jax.ShapeDtypeStruct((rows, width), BF16),
            jax.ShapeDtypeStruct((2 * rows, ff), BF16),
            jax.ShapeDtypeStruct((ff, width), BF16),
            jax.ShapeDtypeStruct((8, rows), F32),
        ),
        in_specs=[vmem] * 3,
        out_specs=(vmem, vmem, pl.BlockSpec(memory_space=pl.ANY), vmem),
        scratch_shapes=[
            pltpu.VMEM((rows_all, ff), BF16),
            pltpu.VMEM((rows_all, width), BF16),
            pltpu.VMEM((rows_all, width), BF16),
            pltpu.VMEM((3, rows_all, width // 4), BF16),
            pltpu.VMEM((rows_all, width // 4), BF16),
            pltpu.VMEM((rows_all, ff), BF16),
            pltpu.VMEM((rows_all, ff // 2), BF16),
            pltpu.VMEM((ff, width), BF16),
            pltpu.VMEM((8, rows), F32),
            pltpu.VMEM((3, 8, rows), F32),
            dma((32,)), dma((32,)), dma((4,)), dma((4,)),
            dma((4, 3)), dma((4, 3)), dma((4,)), dma((4,)),
            dma((4, 3)), dma((4, 3)), dma((4,)), dma((4,)),
            dma((32,)), dma((32,)), dma((2,)), dma((8,)), dma((3,)), dma((3,)),
        ],
        compiler_params=pltpu.CompilerParams(
            collective_id=0, has_side_effects=True, vmem_limit_bytes=62 * 1024 * 1024
        ),
        cost_estimate=pl.CostEstimate(
            flops=6 * rows_all * ff * width, bytes_accessed=30000000, transcendentals=0
        ),
    )(hs, gs, w)


def per_device(gate_pre, up_pre, out_grad, combine, expert_ids, down_weight):
    tokens = gate_pre.shape[0]
    x = lax.axis_index("hid")
    width = down_weight.shape[2]
    quarter = width // 4
    rows = E * CAP
    flat = jnp.concatenate([expert_ids[:, 0], expert_ids[:, 1]])
    onehot = (flat[:, None] == jnp.arange(E, dtype=jnp.int32)[None, :]).astype(BF16)
    count = tokens * TOP
    before = (jnp.arange(count)[:, None] > jnp.arange(count)[None, :]).astype(BF16)
    earlier = jnp.dot(before, onehot, preferred_element_type=F32)
    position = jnp.sum(earlier * onehot.astype(F32), axis=1).astype(jnp.int32)
    target = flat * CAP + position
    row_ids = jnp.arange(rows, dtype=jnp.int32)
    pack = (target[None, :] == row_ids[:, None]).astype(BF16)
    hit = target[:, None] == row_ids[None, :]
    unpack = hit.astype(BF16)

    gate_f = gate_pre.astype(F32)
    up_f = up_pre.astype(F32)
    sig = jax.nn.sigmoid(gate_f)
    hidden = (gate_f * sig * up_f).astype(BF16)
    hs = (
        jnp.dot(pack[:, :tokens], hidden[:, 0], preferred_element_type=F32)
        + jnp.dot(pack[:, tokens:], hidden[:, 1], preferred_element_type=F32)
    ).astype(BF16)
    mine = jnp.concatenate(
        [
            lax.dynamic_slice_in_dim(out_grad, j * width + x * quarter, quarter, axis=1)
            for j in range(4)
        ],
        axis=1,
    ).astype(F32)
    scaled0 = (combine[:, 0:1] * mine).astype(BF16)
    scaled1 = (combine[:, 1:2] * mine).astype(BF16)
    gs = (
        jnp.dot(pack[:, :tokens], scaled0, preferred_element_type=F32)
        + jnp.dot(pack[:, tokens:], scaled1, preferred_element_type=F32)
    ).astype(BF16)

    oh, bh, wg, cg = exchange(hs, gs, down_weight[0])

    mixed = (
        combine[:, 0:1] * jnp.dot(unpack[:tokens], oh, preferred_element_type=F32)
        + combine[:, 1:2] * jnp.dot(unpack[tokens:], oh, preferred_element_type=F32)
    ).astype(BF16).reshape(tokens, 4, quarter)
    slot_cg = jnp.sum(jnp.where(hit, cg[0:1, :], 0.0), axis=1)
    combine_grad = jnp.stack([slot_cg[:tokens], slot_cg[tokens:]], axis=1) / combine
    both = jnp.concatenate([unpack, unpack], axis=1)
    hidden_grad = jnp.stack(
        [
            jnp.dot(both[:tokens], bh, preferred_element_type=F32),
            jnp.dot(both[tokens:], bh, preferred_element_type=F32),
        ],
        axis=1,
    )
    gate_grad = (hidden_grad * up_f * sig * (1.0 + gate_f * (1.0 - sig))).astype(BF16)
    up_grad = (hidden_grad * gate_f * sig).astype(BF16)
    return mixed, combine_grad, gate_grad, up_grad, wg[None]


def solution(mesh):
    return jax.shard_map(
        per_device,
        mesh=mesh,
        in_specs=(
            P("dp", None, "hid"),
            P("dp", None, "hid"),
            P("dp", None),
            P("dp", None),
            P("dp", None),
            P("dp", "hid", None),
        ),
        out_specs=(
            P("dp", None, "hid"),
            P("dp", None),
            P("dp", None, "hid"),
            P("dp", None, "hid"),
            P("dp", "hid", None),
        ),
        check_vma=False,
    )
```

time: 1010 us -> 188 us (0.19); the launches traced: 995 us -> 188 us
  local copies, waits for them, and re-layouts: 417 us -> 9.5 us
  blocking collectives: 276 us -> 0 us
  waiting for transfers between devices: 195 us -> 0 us
  Pallas kernels: 0 us -> 163 us
  other arithmetic: 42 us -> 4.87 us
  matrix products: 44.5 us -> 8.85 us
  between operations: 14.6 us -> 0.86 us
    unnamed x24 -> x23, local copies, waits for them, and re-layouts: 349 us -> 6.85 us
    all_to_all x3 -> x0, blocking collectives: 264 us -> none  [the longest x1 112 us: per_device(): lax.all_to_all(expert_out.reshape(dp_count, capacity, slice_width), 'dp',...]
    pallas_call x0 -> x1, Pallas kernels: none -> 163 us  [exchange(): pl.pallas_call(exchange_kernel, out_shape=(jax.ShapeDtypeStruct((rows, wi...]
    all_to_all x1 -> x0, waiting for transfers between devices: 151 us -> none  [per_device(): lax.all_to_all(partial_back, 'dp', split_axis=0, concat_axis=0, tiled=True)]
    gather x6 -> x0, local copies, waits for them, and re-layouts: 55.7 us -> none  [the longest x2 23.6 us: per_device(): jnp.take(back_grad.reshape(dp_count * capacity, local_ff), return_index,...]
    unnamed x2 -> x0, waiting for transfers between devices: 43.9 us -> none
    dot_general x3 -> x9, matrix products: 44.5 us -> 8.85 us  [the longest x1 1.78 us: per_device(): jnp.dot(unpack[:tokens], oh, preferred_element_type=F32)]
    reduce_sum x5 -> x1, other arithmetic: 14.3 us -> 0.19 us  [per_device(): slot_cg = jnp.sum(jnp.where(hit, cg[0:1, :], 0.0), axis=1)]
  transfers between devices with their start and end apart: 2 -> 0, of which waited for: 2 -> 0; matrix products, arithmetic and copies ran while one was open for 2% -> 0% of each run, Pallas kernels for 0% -> 0%
where the time goes in v1:
time: 188 us
  Pallas kernels  163 us (87%)
  local copies, waits for them, and re-layouts  9.5 us (5%)
  matrix products  8.85 us (5%)
  other arithmetic  4.87 us (3%)
    pallas_call x1, Pallas kernels, exchange(): pl.pallas_call(exchange_kernel, out_shape=(jax.ShapeDtypeStruct((rows, wi...  163 us
    unnamed x23, local copies, waits for them, and re-layouts  6.85 us

profile of v1, /device:TPU:1, one launch (start us, length us, event | category | flops | bytes accessed | tf_op | source)
XLA Modules:
  0.0 187.5 jit_solution(3855513590578169568)
XLA Ops:
  0.6 0.0 copy-start.7
  0.6 2.6 %fusion.3 = bf16[128,2,2048]{2,0,1:T(8,128)(2,1)S(1)} fusion(bf16[128,2,2048]{2,1,0:T(2,128)(2,1)} %param.7, bf16[128,2,2048]{2,1,0:T(2,128)(2,1)} %param.6), kind=kLoop, calls=%fused_computation.15 | loop fusion | flops 4194304 | bytes 3145728 | tf_op jit(solution)/shard_map/convert_element_type | solution.py:411
  3.2 0.0 copy-done.7
  3.2 0.2 fusion.13
  3.5 0.1 iota_compare_fusion
  3.5 0.6 fusion.16
  4.1 0.0 copy-start.6
  4.1 1.7 add_convert_fusion.hs
  5.8 0.0 copy-done.6
  5.8 1.1 constant_dynamic-slice_fusion.3
  6.9 0.5 fusion.18
  7.4 1.6 fusion.gs
  9.0 163.4 %shard_map.101 = (bf16[384,1536]{1,0:T(8,128)(2,1)}, bf16[768,2048]{1,0:T(8,128)(2,1)}, bf16[2048,1536]{1,0:T(8,128)(2,1)}, f32[8,384]{1,0:T(8,128)}) custom-call(bf16[384,2048]{1,0:T(8,128)(2,1)} %add_convert_fusion.hs, bf16[384,1536]{1,0:T(8,128)(2,1)} %fusion.gs, bf16[2048,1536]{1,0:T(8,128)(2,1)} %bitcast.31), custom_call_target="tpu_custom_call" | custom-call | flops 28991029248 | bytes 30000000 | tf_op jit(solution)/shard_map/pallas_call | solution.py:355
  172.5 0.0 copy-start.1
  172.5 0.1 iota_compare_fusion.1
  172.6 0.0 copy-start.4
  172.6 1.8 convolution_multiply_fusion.1
  174.4 0.0 copy-done.4
  174.4 0.0 copy-done.1
  174.4 0.0 copy-start
  174.4 0.4 fusion.2
  174.8 0.8 reshape.54
  175.7 0.7 slice_reduce_fusion
  176.4 0.2 select_reduce_fusion
  176.6 0.6 maximum_divide_fusion
  177.2 0.0 copy-done
  177.2 0.0 copy-start.5
  177.2 0.0 copy-start.2
  177.2 0.0 copy-start.3
  177.2 1.6 convolution_bitcast_fusion
  178.7 0.0 copy-done.5
  178.7 0.0 slice-start
  178.7 0.6 convolution_bitcast_fusion.1
  179.3 0.0 copy-done.2
  179.3 0.0 copy-done.3
  179.3 0.0 slice-start.1
  179.4 1.4 fusion.12
  180.7 2.0 %copy.17 = bf16[128,2,2048]{2,1,0:T(2,128)(2,1)} copy(bf16[128,2,2048]{2,0,1:T(8,128)(2,1)S(1)} %get-tuple-element.24) | data formatting | bytes 2097152
  182.8 2.0 %copy.18 = bf16[128,2,2048]{2,1,0:T(2,128)(2,1)} copy(bf16[128,2,2048]{2,0,1:T(8,128)(2,1)S(1)} %get-tuple-element.23) | data formatting | bytes 2097152
  184.8 0.0 slice-done
  184.8 0.0 slice-done.1
  184.8 2.7 %copy.29 = bf16[1,2048,1536]{2,1,0:T(8,128)(2,1)} copy(bf16[1,2048,1536]{2,1,0:T(8,128)(2,1)S(1)} %bitcast.30) | data formatting | bytes 12582912
  (6 shorter events, 0.0 us)
Async XLA Ops:
  0.6 2.6 %copy-start.7 = (s32[128,2]{0,1:T(2,128)S(1)}, s32[128,2]{0,1:T(2,128)}, u32[]{:S(2)}) copy-start(s32[128,2]{0,1:T(2,128)} %param.10) | copy-start | bytes 3076
  4.1 1.7 copy-start.6
  172.5 2.0 %copy-start.1 = (bf16[384,1536]{1,0:T(8,128)(2,1)S(1)}, bf16[384,1536]{1,0:T(8,128)(2,1)}, u32[]{:S(2)}) copy-start(bf16[384,1536]{1,0:T(8,128)(2,1)} %get-tuple-element.9) | copy-start | bytes 3538948
  172.6 1.8 copy-start.4
  174.4 2.7 %copy-start = (bf16[768,2048]{1,0:T(8,128)(2,1)S(1)}, bf16[768,2048]{1,0:T(8,128)(2,1)}, u32[]{:S(2)}) copy-start(bf16[768,2048]{1,0:T(8,128)(2,1)} %get-tuple-element.11) | copy-start | bytes 9437188
  177.2 1.6 copy-start.5
  177.2 2.2 %copy-start.2 = (bf16[128,2,2048]{2,1,0:T(2,128)(2,1)S(1)}, bf16[128,2,2048]{2,1,0:T(2,128)(2,1)}, u32[]{:S(2)}) copy-start(bf16[128,2,2048]{2,1,0:T(2,128)(2,1)} %param.7) | copy-start | bytes 3145732
  177.2 2.2 %copy-start.3 = (bf16[128,2,2048]{2,1,0:T(2,128)(2,1)S(1)}, bf16[128,2,2048]{2,1,0:T(2,128)(2,1)}, u32[]{:S(2)}) copy-start(bf16[128,2,2048]{2,1,0:T(2,128)(2,1)} %param.6) | copy-start | bytes 3145732
  178.7 6.1 %slice-start = ((s8[6291456]{0:T(1024)(128)(4,1)}), s8[4194304]{0:T(1024)(128)(4,1)S(1)}, s32[]{:S(2)}) async-start(s8[6291456]{0:T(1024)(128)(4,1)} %bitcast.28), calls=%async_computation | async-start | bytes 8388608
  179.3 5.5 %slice-start.1 = ((s8[6291456]{0:T(1024)(128)(4,1)}), s8[2097152]{0:T(1024)(128)(4,1)S(1)}, s32[]{:S(2)}) async-start(s8[6291456]{0:T(1024)(128)(4,1)} %bitcast.28), calls=%async_computation.1 | async-start | bytes 4194304

commit v2 on v1

--- a/solution.py
+++ b/solution.py
@@ -14,16 +14,16 @@
 
 
 def exchange_kernel(
-    hs, gs, w, oh, bh, wg, cg,
-    hr, gr, os, orx, od, bs, br, wt, cgs, cgr,
+    hs, gs, w_hbm, oh, bh, wg, cg,
+    w, hr, gr, os, orx, od, bs, br, wt, cgs, cgr,
     send_h, send_g, recv_h, recv_g, xg_send, xg_recv, sib_send, sib_recv,
     xo_send, xo_recv, bsib_send, bsib_recv, home_o_send, home_b_send,
-    home_recv, wg_sem, cg_send, cg_recv,
+    home_recv, wg_sem, w_sem, cg_send, cg_recv,
 ):
     me = lax.axis_index("dp")
     x = lax.axis_index("hid")
     z = lax.div(me, 8)
-    yc = lax.rem(me, 8)
+    y = lax.rem(lax.div(me, 2), 4)
     core = lax.rem(me, 2)
     e_me = lax.div(me, 4)
     j_me = lax.rem(me, 4)
@@ -35,6 +35,9 @@
     def m(v, k):
         return pl.multiple_of(v, k)
 
+    w_copy = pltpu.make_async_copy(w_hbm, w, w_sem)
+    w_copy.start()
+
     barrier = pltpu.get_barrier_semaphore()
 
     def greet_dp(n, carry):
@@ -52,33 +55,41 @@
     my_half = m(core * half_w, 128)
     other_half = m((1 - core) * half_w, 128)
     my_quarter = m(x * q_w, 128)
-    my_rows = m(me * CAP, 16)
     my_expert_rows = m(e_me * CAP, 16)
 
     def base_of(r):
-        return m(lax.rem(z - r + 4, 4) * rows_n, 16)
-
-    def partner(n):
-        return lax.rem(z + lax.div(n, 8), 4) * 8 + lax.rem(yc + lax.rem(n, 8), 8)
+        return m(r * rows_n, 16)
+
+    def partner(n, sign):
+        dz = lax.rem(n, 4)
+        dy = lax.rem(dz + lax.div(n, 8), 4)
+        dc = lax.rem(lax.div(n, 4), 2)
+        pz = lax.rem(z + sign * dz + 4, 4)
+        py = lax.rem(y + sign * dy + 4, 4)
+        return pz * 8 + py * 2 + lax.rem(core + dc, 2)
+
+    def slot_rows(n, source_core):
+        slot = lax.div(n, 8) * 8 + source_core * 4 + lax.rem(n, 4)
+        return pl.ds(m(slot * CAP, 16), CAP)
 
     pltpu.make_async_copy(
         gs.at[pl.ds(my_expert_rows, CAP), pl.ds(m(j_me * q_w, 128), q_w)],
-        gr.at[pl.ds(my_rows, CAP), pl.ds(my_quarter, q_w)],
+        gr.at[slot_rows(0, core), pl.ds(my_quarter, q_w)],
         recv_g.at[0],
     ).start()
     pltpu.make_async_copy(
         hs.at[pl.ds(my_expert_rows, CAP), pl.ds(my_half, half_w)],
-        hr.at[pl.ds(my_rows, CAP), pl.ds(my_half, half_w)],
+        hr.at[slot_rows(0, core), pl.ds(my_half, half_w)],
         recv_h.at[0],
     ).start()
 
     def g_copy(n):
-        p = partner(n)
+        p = partner(n, 1)
         return pltpu.make_async_remote_copy(
             src_ref=gs.at[
                 pl.ds(m(lax.div(p, 4) * CAP, 16), CAP), pl.ds(m(lax.rem(p, 4) * q_w, 128), q_w)
             ],
-            dst_ref=gr.at[pl.ds(my_rows, CAP), pl.ds(my_quarter, q_w)],
+            dst_ref=gr.at[slot_rows(n, core), pl.ds(my_quarter, q_w)],
             send_sem=send_g.at[n],
             recv_sem=recv_g.at[lax.div(n, 8)],
             device_id=(p, x),
@@ -86,11 +97,11 @@
         )
 
     def h_copy(n):
-        p = partner(n)
+        p = partner(n, 1)
         cols = pl.ds(m(lax.rem(p, 2) * half_w, 128), half_w)
         return pltpu.make_async_remote_copy(
             src_ref=hs.at[pl.ds(m(lax.div(p, 4) * CAP, 16), CAP), cols],
-            dst_ref=hr.at[pl.ds(my_rows, CAP), cols],
+            dst_ref=hr.at[slot_rows(n, core), cols],
             send_sem=send_h.at[n],
             recv_sem=recv_h.at[lax.div(n, 8)],
             device_id=(p, x),
@@ -104,8 +115,15 @@
 
         lax.fori_loop(lo, hi, step, 0)
 
-    loop(1, 32, lambda n: g_copy(n).start())
-    loop(1, 32, lambda n: h_copy(n).start())
+    loop(1, 16, lambda n: g_copy(n).start())
+    loop(1, 8, lambda n: h_copy(n).start())
+
+    def issue(r):
+        loop(r * 8, r * 8 + 8, lambda n: g_copy(n).start())
+        loop(r * 8 - 8, r * 8, lambda n: h_copy(n).start())
+
+    loop(2, 4, issue)
+    loop(24, 32, lambda n: h_copy(n).start())
 
     def xg_copy(r, o):
         part = gr.at[pl.ds(base_of(r), rows_n), pl.ds(my_quarter, q_w)]
@@ -126,8 +144,6 @@
         for o in range(1, 4):
             xg_copy(r, o).start()
 
-    loop(0, 4, pass_g)
-
     def sib_copy(r):
         part = hr.at[pl.ds(base_of(r), rows_n), pl.ds(my_half, half_w)]
         return pltpu.make_async_remote_copy(
@@ -162,15 +178,6 @@
         loop(0, 2, tile)
         for o in range(1, 4):
             xo_copy(r, o).start()
-
-    pass_h(0)
-
-    def h_step(r):
-        pass_h(r + 1)
-        out_product(r)
-
-    loop(0, 3, h_step)
-    out_product(3)
 
     def bsib_copy(r):
         rows = pl.ds(base_of(r), rows_n)
@@ -197,9 +204,9 @@
         bsib_copy(r).start()
 
     def home_b_copy(n):
-        p = lax.rem(z - lax.div(n, 8) + 4, 4) * 8 + lax.rem(yc + lax.rem(n, 8), 8)
-        return pltpu.make_async_remote_copy(
-            src_ref=br.at[pl.ds(m(p * CAP, 16), CAP), :],
+        p = partner(n, -1)
+        return pltpu.make_async_remote_copy(
+            src_ref=br.at[slot_rows(n, lax.rem(p, 2)), :],
             dst_ref=bh.at[
                 pl.ds(m((lax.div(j_me, 2) * E + e_me) * CAP, 16), CAP), pl.ds(my_half, half_w)
             ],
@@ -208,9 +215,9 @@
         )
 
     def home_o_copy(n):
-        p = lax.rem(z - lax.div(n, 8) + 4, 4) * 8 + lax.rem(yc + lax.rem(n, 8), 8)
-        return pltpu.make_async_remote_copy(
-            src_ref=od.at[pl.ds(m(p * CAP, 16), CAP), :],
+        p = partner(n, -1)
+        return pltpu.make_async_remote_copy(
+            src_ref=od.at[slot_rows(n, lax.rem(p, 2)), :],
             dst_ref=oh.at[pl.ds(my_expert_rows, CAP), pl.ds(m(j_me * q_w, 128), q_w)],
             send_sem=home_o_send.at[n], recv_sem=home_recv.at[0],
             device_id=(p, x), device_id_type=MESH,
@@ -242,32 +249,6 @@
 
         loop(0, 8, tile)
 
-    def back_first():
-        back_sum(0)
-        pltpu.make_async_copy(
-            br.at[pl.ds(my_rows, CAP), :],
-            bh.at[
-                pl.ds(m((lax.div(j_me, 2) * E + e_me) * CAP, 16), CAP), pl.ds(my_half, half_w)
-            ],
-            home_recv.at[1],
-        ).start()
-        loop(1, 8, lambda n: home_b_copy(n).start())
-
-    def back_next(r):
-        back_sum(r)
-        loop(r * 8, r * 8 + 8, lambda n: home_b_copy(n).start())
-
-    back_product(0)
-    back_product(1)
-    back_first()
-
-    def b_step(r):
-        back_product(r + 1)
-        back_next(r)
-
-    loop(1, 3, b_step)
-    back_next(3)
-
     def wg_copy(n):
         rows = pl.ds(m(n * 256, 16), 256)
         return pltpu.make_async_copy(wt.at[rows, :], wg.at[rows, :], wg_sem.at[n])
@@ -280,22 +261,64 @@
         wt[pl.ds(m(n * 256, 16), 256), :] = acc.astype(BF16)
         wg_copy(n).start()
 
-    def out_first():
-        out_sum(0)
-        pltpu.make_async_copy(
-            od.at[pl.ds(my_rows, CAP), :],
-            oh.at[pl.ds(my_expert_rows, CAP), pl.ds(m(j_me * q_w, 128), q_w)],
-            home_recv.at[0],
-        ).start()
-        loop(1, 8, lambda n: home_o_copy(n).start())
-
-    def out_next(r):
+    def home_b(r):
+        back_sum(r)
+
+        @pl.when(r == 0)
+        def _():
+            pltpu.make_async_copy(
+                br.at[slot_rows(0, core), :],
+                bh.at[
+                    pl.ds(m((lax.div(j_me, 2) * E + e_me) * CAP, 16), CAP), pl.ds(my_half, half_w)
+                ],
+                home_recv.at[1],
+            ).start()
+
+        loop(jnp.maximum(r * 8, 1), r * 8 + 8, lambda n: home_b_copy(n).start())
+
+    def home_o(r):
         out_sum(r)
-        loop(r * 8, r * 8 + 8, lambda n: home_o_copy(n).start())
-
-    loop(0, 8, wg_tile)
-    out_first()
-    loop(1, 4, out_next)
+
+        @pl.when(r == 0)
+        def _():
+            pltpu.make_async_copy(
+                od.at[slot_rows(0, core), :],
+                oh.at[pl.ds(my_expert_rows, CAP), pl.ds(m(j_me * q_w, 128), q_w)],
+                home_recv.at[0],
+            ).start()
+
+        loop(jnp.maximum(r * 8, 1), r * 8 + 8, lambda n: home_o_copy(n).start())
+
+    pass_g(0)
+    w_copy.wait()
+
+    def step(r):
+        @pl.when(r < 3)
+        def _():
+            pass_g(r + 1)
+
+        @pl.when(r < 4)
+        def _():
+            pass_h(r)
+
+        @pl.when((r > 0) & (r < 5))
+        def _():
+            home_b(r - 1)
+
+        @pl.when(r > 1)
+        def _():
+            home_o(r - 2)
+
+        @pl.when(r < 4)
+        def _():
+            out_product(r)
+            back_product(r)
+
+        @pl.when(r > 3)
+        def _():
+            loop(r * 4 - 16, r * 4 - 12, wg_tile)
+
+    loop(0, 6, step)
 
     pltpu.make_async_copy(oh, oh, home_recv.at[0]).wait()
     fold = jnp.zeros((rows_n, 128), F32)
@@ -360,9 +383,10 @@
             jax.ShapeDtypeStruct((ff, width), BF16),
             jax.ShapeDtypeStruct((8, rows), F32),
         ),
-        in_specs=[vmem] * 3,
+        in_specs=[vmem, vmem, pl.BlockSpec(memory_space=pl.ANY)],
         out_specs=(vmem, vmem, pl.BlockSpec(memory_space=pl.ANY), vmem),
         scratch_shapes=[
+            pltpu.VMEM((ff, width), BF16),
             pltpu.VMEM((rows_all, ff), BF16),
             pltpu.VMEM((rows_all, width), BF16),
             pltpu.VMEM((rows_all, width), BF16),
@@ -376,7 +400,7 @@
             dma((32,)), dma((32,)), dma((4,)), dma((4,)),
             dma((4, 3)), dma((4, 3)), dma((4,)), dma((4,)),
             dma((4, 3)), dma((4, 3)), dma((4,)), dma((4,)),
-            dma((32,)), dma((32,)), dma((2,)), dma((8,)), dma((3,)), dma((3,)),
+            dma((32,)), dma((32,)), dma((2,)), dma((8,)), dma, dma((3,)), dma((3,)),
         ],
         compiler_params=pltpu.CompilerParams(
             collective_id=0, has_side_effects=True, vmem_limit_bytes=62 * 1024 * 1024

time: 188 us -> 161 us (0.86)
  Pallas kernels: 163 us -> 136 us
    pallas_call x1, Pallas kernels: 163 us -> 136 us  [exchange(): pl.pallas_call(exchange_kernel, out_shape=(jax.ShapeDtypeStruct((rows, wi...]
where the time goes in v2:
time: 161 us
  Pallas kernels  136 us (84%)
  local copies, waits for them, and re-layouts  9.5 us (6%)
  matrix products  8.86 us (6%)
  other arithmetic  4.87 us (3%)
    pallas_call x1, Pallas kernels, exchange(): pl.pallas_call(exchange_kernel, out_shape=(jax.ShapeDtypeStruct((rows, wi...  136 us
    unnamed x23, local copies, waits for them, and re-layouts  6.85 us

profile of v2, /device:TPU:1, one launch (start us, length us, event | category | flops | bytes accessed | tf_op | source)
XLA Modules:
  0.0 160.6 jit_solution(15041936215092216030)
XLA Ops:
  0.6 0.0 copy-start.7
  0.6 2.6 %fusion.3 = bf16[128,2,2048]{2,0,1:T(8,128)(2,1)S(1)} fusion(bf16[128,2,2048]{2,1,0:T(2,128)(2,1)} %param.7, bf16[128,2,2048]{2,1,0:T(2,128)(2,1)} %param.6), kind=kLoop, calls=%fused_computation.15 | loop fusion | flops 4194304 | bytes 3145728 | tf_op jit(solution)/shard_map/convert_element_type | solution.py:435
  3.2 0.0 copy-done.7
  3.2 0.2 fusion.13
  3.5 0.1 iota_compare_fusion
  3.5 0.6 fusion.16
  4.1 0.0 copy-start.6
  4.1 1.7 %add_convert_fusion.hs = bf16[384,2048]{1,0:T(8,128)(2,1)} fusion(f32[384,2048]{1,0:T(8,128)S(1)} %fusion.16, bf16[128,2,2048]{2,0,1:T(8,128)(2,1)S(1)} %fusion.3, pred[384,256]{1,0:T(32,128)(4,1)S(1)} %iota_compare_fusion), kind=kOutput, calls=%fused_computation.4 | convolution fusion | flops 202899456 | bytes 5292032 | tf_op jit(solution)/shard_map/dot_general | solution.py:438
  5.8 0.0 copy-done.6
  5.8 1.1 constant_dynamic-slice_fusion.3
  6.9 0.5 fusion.18
  7.4 1.6 fusion.gs
  9.0 136.5 %shard_map.101 = (bf16[384,1536]{1,0:T(8,128)(2,1)}, bf16[768,2048]{1,0:T(8,128)(2,1)}, bf16[2048,1536]{1,0:T(8,128)(2,1)}, f32[8,384]{1,0:T(8,128)}) custom-call(bf16[384,2048]{1,0:T(8,128)(2,1)} %add_convert_fusion.hs, bf16[384,1536]{1,0:T(8,128)(2,1)} %fusion.gs, bf16[2048,1536]{1,0:T(8,128)(2,1)} %bitcast.31), custom_call_target="tpu_custom_call" | custom-call | flops 28991029248 | bytes 30000000 | tf_op jit(solution)/shard_map/pallas_call | solution.py:378
  145.5 0.0 copy-start.1
  145.5 0.1 iota_compare_fusion.1
  145.6 0.0 copy-start.4
  145.6 1.8 %convolution_multiply_fusion.1 = f32[128,1536]{1,0:T(8,128)S(1)} fusion(bf16[384,1536]{1,0:T(8,128)(2,1)} %get-tuple-element.9, f32[128]{0:T(128)S(1)} %get-tuple-element.32, pred[256,384]{1,0:T(32,128)(4,1)S(1)} %iota_compare_fusion.1), kind=kOutput, calls=%fused_computation.11 | convolution fusion | flops 151191552 | bytes 2015744 | tf_op jit(solution)/shard_map/dot_general | solution.py:457
  147.4 0.0 copy-done.4
  147.4 0.0 copy-done.1
  147.4 0.0 copy-start
  147.5 0.4 fusion.2
  147.8 0.8 reshape.54
  148.7 0.7 slice_reduce_fusion
  149.4 0.2 select_reduce_fusion
  149.6 0.6 maximum_divide_fusion
  150.2 0.0 copy-done
  150.2 0.0 copy-start.5
  150.2 0.0 copy-start.2
  150.2 0.0 copy-start.3
  150.2 1.6 convolution_bitcast_fusion
  151.8 0.0 copy-done.5
  151.8 0.0 slice-start
  151.8 0.6 convolution_bitcast_fusion.1
  152.4 0.0 copy-done.2
  152.4 0.0 copy-done.3
  152.4 0.0 slice-start.1
  152.4 1.4 fusion.12
  153.8 2.0 %copy.17 = bf16[128,2,2048]{2,1,0:T(2,128)(2,1)} copy(bf16[128,2,2048]{2,0,1:T(8,128)(2,1)S(1)} %get-tuple-element.24) | data formatting | bytes 2097152
  155.8 2.0 %copy.18 = bf16[128,2,2048]{2,1,0:T(2,128)(2,1)} copy(bf16[128,2,2048]{2,0,1:T(8,128)(2,1)S(1)} %get-tuple-element.23) | data formatting | bytes 2097152
  157.9 0.0 slice-done
  157.9 0.0 slice-done.1
  157.9 2.7 %copy.29 = bf16[1,2048,1536]{2,1,0:T(8,128)(2,1)} copy(bf16[1,2048,1536]{2,1,0:T(8,128)(2,1)S(1)} %bitcast.30) | data formatting | bytes 12582912
  (6 shorter events, 0.0 us)
Async XLA Ops:
  0.6 2.6 %copy-start.7 = (s32[128,2]{0,1:T(2,128)S(1)}, s32[128,2]{0,1:T(2,128)}, u32[]{:S(2)}) copy-start(s32[128,2]{0,1:T(2,128)} %param.10) | copy-start | bytes 3076
  4.1 1.7 %copy-start.6 = (f32[128,2]{0,1:T(2,128)S(1)}, f32[128,2]{0,1:T(2,128)}, u32[]{:S(2)}) copy-start(f32[128,2]{0,1:T(2,128)} %param.9) | copy-start | bytes 3076
  145.5 2.0 %copy-start.1 = (bf16[384,1536]{1,0:T(8,128)(2,1)S(1)}, bf16[384,1536]{1,0:T(8,128)(2,1)}, u32[]{:S(2)}) copy-start(bf16[384,1536]{1,0:T(8,128)(2,1)} %get-tuple-element.9) | copy-start | bytes 3538948
  145.6 1.8 %copy-start.4 = (pred[256,384]{1,0:T(32,128)(4,1)}, pred[256,384]{1,0:T(32,128)(4,1)S(1)}, u32[]{:S(2)}) copy-start(pred[256,384]{1,0:T(32,128)(4,1)S(1)} %iota_compare_fusion.1) | copy-start | bytes 294916
  147.4 2.7 %copy-start = (bf16[768,2048]{1,0:T(8,128)(2,1)S(1)}, bf16[768,2048]{1,0:T(8,128)(2,1)}, u32[]{:S(2)}) copy-start(bf16[768,2048]{1,0:T(8,128)(2,1)} %get-tuple-element.11) | copy-start | bytes 9437188
  150.2 1.6 copy-start.5
  150.2 2.2 %copy-start.2 = (bf16[128,2,2048]{2,1,0:T(2,128)(2,1)S(1)}, bf16[128,2,2048]{2,1,0:T(2,128)(2,1)}, u32[]{:S(2)}) copy-start(bf16[128,2,2048]{2,1,0:T(2,128)(2,1)} %param.7) | copy-start | bytes 3145732
  150.2 2.2 %copy-start.3 = (bf16[128,2,2048]{2,1,0:T(2,128)(2,1)S(1)}, bf16[128,2,2048]{2,1,0:T(2,128)(2,1)}, u32[]{:S(2)}) copy-start(bf16[128,2,2048]{2,1,0:T(2,128)(2,1)} %param.6) | copy-start | bytes 3145732
  151.8 6.1 %slice-start = ((s8[6291456]{0:T(1024)(128)(4,1)}), s8[4194304]{0:T(1024)(128)(4,1)S(1)}, s32[]{:S(2)}) async-start(s8[6291456]{0:T(1024)(128)(4,1)} %bitcast.28), calls=%async_computation | async-start | bytes 8388608
  152.4 5.5 %slice-start.1 = ((s8[6291456]{0:T(1024)(128)(4,1)}), s8[2097152]{0:T(1024)(128)(4,1)S(1)}, s32[]{:S(2)}) async-start(s8[6291456]{0:T(1024)(128)(4,1)} %bitcast.28), calls=%async_computation.1 | async-start | bytes 4194304

commit v3 on v2

--- a/solution.py
+++ b/solution.py
@@ -15,9 +15,9 @@
 
 def exchange_kernel(
     hs, gs, w_hbm, oh, bh, wg, cg,
-    w, hr, gr, os, orx, od, bs, br, wt, cgs, cgr,
-    send_h, send_g, recv_h, recv_g, xg_send, xg_recv, sib_send, sib_recv,
-    xo_send, xo_recv, bsib_send, bsib_recv, home_o_send, home_b_send,
+    w, hr, gr, os, opx, orx, od, bs, br, wt, cgs, cgr,
+    send_h, send_g, recv_h, recv_g, xg_send, xg_recv, xf_send, xf_recv, sib_send, sib_recv,
+    xp_send, xp_recv, xo_send, xo_recv, bsib_send, bsib_recv, home_o_send, home_b_send,
     home_recv, wg_sem, w_sem, cg_send, cg_recv,
 ):
     me = lax.axis_index("dp")
@@ -125,24 +125,44 @@
     loop(2, 4, issue)
     loop(24, 32, lambda n: h_copy(n).start())
 
-    def xg_copy(r, o):
-        part = gr.at[pl.ds(base_of(r), rows_n), pl.ds(my_quarter, q_w)]
+    half_rows = rows_n // 2
+
+    def neighbour(d):
+        return lax.rem(x + (1, 3)[d], 4)
+
+    def quarter_at(offset):
+        return pl.ds(m(lax.rem(x + offset, 4) * q_w, 128), q_w)
+
+    def half_of(r, d):
+        return pl.ds(m(r * rows_n + d * half_rows, 16), half_rows)
+
+    def xg_copy(r, d):
+        part = gr.at[pl.ds(base_of(r), rows_n), quarter_at(0)]
         return pltpu.make_async_remote_copy(
             src_ref=part, dst_ref=part,
-            send_sem=xg_send.at[r, o - 1], recv_sem=xg_recv.at[r, o - 1],
-            device_id=(me, lax.rem(x + o, 4)), device_id_type=MESH,
-        )
-
-    def xg_wait(r, o):
-        cols = m(lax.rem(x - o + 4, 4) * q_w, 128)
-        part = gr.at[pl.ds(base_of(r), rows_n), pl.ds(cols, q_w)]
-        pltpu.make_async_copy(part, part, xg_recv.at[r, o - 1]).wait()
+            send_sem=xg_send.at[r, d], recv_sem=xg_recv.at[r, d],
+            device_id=(me, neighbour(d)), device_id_type=MESH,
+        )
+
+    def xf_copy(r, d):
+        part = gr.at[half_of(r, d), quarter_at((3, 1)[d])]
+        return pltpu.make_async_remote_copy(
+            src_ref=part, dst_ref=part,
+            send_sem=xf_send.at[r, d], recv_sem=xf_recv.at[r, d],
+            device_id=(me, neighbour(d)), device_id_type=MESH,
+        )
 
     def pass_g(r):
-        part = gr.at[pl.ds(base_of(r), rows_n), pl.ds(my_quarter, q_w)]
+        part = gr.at[pl.ds(base_of(r), rows_n), quarter_at(0)]
         pltpu.make_async_copy(part, part, recv_g.at[r]).wait()
-        for o in range(1, 4):
-            xg_copy(r, o).start()
+        for d in range(2):
+            xg_copy(r, d).start()
+
+    def forward_g(r):
+        for d in range(2):
+            part = gr.at[pl.ds(base_of(r), rows_n), quarter_at((3, 1)[d])]
+            pltpu.make_async_copy(part, part, xg_recv.at[r, d]).wait()
+            xf_copy(r, d).start()
 
     def sib_copy(r):
         part = hr.at[pl.ds(base_of(r), rows_n), pl.ds(my_half, half_w)]
@@ -156,14 +176,35 @@
         pltpu.make_async_copy(part, part, recv_h.at[r]).wait()
         sib_copy(r).start()
 
-    def xo_copy(r, o):
-        peer = lax.rem(x + o, 4)
-        return pltpu.make_async_remote_copy(
-            src_ref=os.at[pl.ds(base_of(r), rows_n), pl.ds(m(peer * q_w, 128), q_w)],
-            dst_ref=orx.at[o - 1, pl.ds(base_of(r), rows_n), :],
-            send_sem=xo_send.at[r, o - 1], recv_sem=xo_recv.at[r, o - 1],
-            device_id=(me, peer), device_id_type=MESH,
-        )
+    def xp_copy(r, d):
+        return pltpu.make_async_remote_copy(
+            src_ref=os.at[half_of(r, d), quarter_at(2)],
+            dst_ref=opx.at[d, pl.ds(m(r * half_rows, 16), half_rows), :],
+            send_sem=xp_send.at[r, d], recv_sem=xp_recv.at[r, d],
+            device_id=(me, neighbour(d)), device_id_type=MESH,
+        )
+
+    def xo_copy(r, d):
+        return pltpu.make_async_remote_copy(
+            src_ref=os.at[pl.ds(base_of(r), rows_n), quarter_at((1, 3)[d])],
+            dst_ref=orx.at[d, pl.ds(base_of(r), rows_n), :],
+            send_sem=xo_send.at[r, d], recv_sem=xo_recv.at[r, d],
+            device_id=(me, neighbour(d)), device_id_type=MESH,
+        )
+
+    def pass_out(r):
+        for d in range(2):
+            part = opx.at[d, pl.ds(m(r * half_rows, 16), half_rows), :]
+            pltpu.make_async_copy(part, part, xp_recv.at[r, d]).wait()
+
+            def tile(i):
+                sub = pl.ds(m(r * rows_n + d * half_rows + i * CAP, 16), CAP)
+                come = opx[d, pl.ds(m(r * half_rows + i * CAP, 16), CAP), :]
+                cols = quarter_at((1, 3)[d])
+                os[sub, cols] = (os[sub, cols].astype(F32) + come.astype(F32)).astype(BF16)
+
+            loop(0, half_rows // CAP, tile)
+            xo_copy(r, d).start()
 
     def out_product(r):
         part = hr.at[pl.ds(base_of(r), rows_n), pl.ds(other_half, half_w)]
@@ -176,8 +217,8 @@
             os[rows, cols] = acc.astype(BF16)
 
         loop(0, 2, tile)
-        for o in range(1, 4):
-            xo_copy(r, o).start()
+        for d in range(2):
+            xp_copy(r, d).start()
 
     def bsib_copy(r):
         rows = pl.ds(base_of(r), rows_n)
@@ -189,8 +230,9 @@
         )
 
     def back_product(r):
-        for o in range(1, 4):
-            xg_wait(r, o)
+        for d in range(2):
+            part = gr.at[half_of(r, d), quarter_at(2)]
+            pltpu.make_async_copy(part, part, xf_recv.at[r, d]).wait()
         rows = pl.ds(base_of(r), rows_n)
 
         def tile(n):
@@ -236,14 +278,14 @@
         loop(0, 8, tile)
 
     def out_sum(r):
-        for o in range(1, 4):
-            part = orx.at[o - 1, pl.ds(base_of(r), rows_n), :]
-            pltpu.make_async_copy(part, part, xo_recv.at[r, o - 1]).wait()
+        for d in range(2):
+            part = orx.at[d, pl.ds(base_of(r), rows_n), :]
+            pltpu.make_async_copy(part, part, xo_recv.at[r, d]).wait()
 
         def tile(i):
             sub = pl.ds(m(base_of(r) + i * CAP, 16), CAP)
             total = os[sub, pl.ds(my_quarter, q_w)].astype(F32)
-            for k in range(3):
+            for k in range(2):
                 total = total + orx[k, sub, :].astype(F32)
             od[sub, :] = total.astype(BF16)
 
@@ -290,12 +332,18 @@
         loop(jnp.maximum(r * 8, 1), r * 8 + 8, lambda n: home_o_copy(n).start())
 
     pass_g(0)
+    pass_g(1)
+    forward_g(0)
     w_copy.wait()
 
     def step(r):
+        @pl.when(r < 2)
+        def _():
+            pass_g(r + 2)
+
         @pl.when(r < 3)
         def _():
-            pass_g(r + 1)
+            forward_g(r + 1)
 
         @pl.when(r < 4)
         def _():
@@ -313,6 +361,7 @@
         def _():
             out_product(r)
             back_product(r)
+            pass_out(r)
 
         @pl.when(r > 3)
         def _():
@@ -362,9 +411,11 @@
     def drain_r(r):
         sib_copy(r).wait_send()
         bsib_copy(r).wait_send()
-        for o in range(1, 4):
-            xg_copy(r, o).wait_send()
-            xo_copy(r, o).wait_send()
+        for d in range(2):
+            xg_copy(r, d).wait_send()
+            xf_copy(r, d).wait_send()
+            xp_copy(r, d).wait_send()
+            xo_copy(r, d).wait_send()
 
     loop(0, 4, drain_r)
 
@@ -390,7 +441,8 @@
             pltpu.VMEM((rows_all, ff), BF16),
             pltpu.VMEM((rows_all, width), BF16),
             pltpu.VMEM((rows_all, width), BF16),
-            pltpu.VMEM((3, rows_all, width // 4), BF16),
+            pltpu.VMEM((2, rows_all // 2, width // 4), BF16),
+            pltpu.VMEM((2, rows_all, width // 4), BF16),
             pltpu.VMEM((rows_all, width // 4), BF16),
             pltpu.VMEM((rows_all, ff), BF16),
             pltpu.VMEM((rows_all, ff // 2), BF16),
@@ -398,8 +450,8 @@
             pltpu.VMEM((8, rows), F32),
             pltpu.VMEM((3, 8, rows), F32),
             dma((32,)), dma((32,)), dma((4,)), dma((4,)),
-            dma((4, 3)), dma((4, 3)), dma((4,)), dma((4,)),
-            dma((4, 3)), dma((4, 3)), dma((4,)), dma((4,)),
+            dma((4, 2)), dma((4, 2)), dma((4, 2)), dma((4, 2)), dma((4,)), dma((4,)),
+            dma((4, 2)), dma((4, 2)), dma((4, 2)), dma((4, 2)), dma((4,)), dma((4,)),
             dma((32,)), dma((32,)), dma((2,)), dma((8,)), dma, dma((3,)), dma((3,)),
         ],
         compiler_params=pltpu.CompilerParams(

time: 161 us -> 152 us (0.944)
  Pallas kernels: 136 us -> 127 us
    pallas_call x1, Pallas kernels: 136 us -> 127 us  [exchange(): pl.pallas_call(exchange_kernel, out_shape=(jax.ShapeDtypeStruct((rows, wi...]
where the time goes in v3:
time: 152 us; the launch traced here: 151 us
  Pallas kernels  127 us (84%)
  local copies, waits for them, and re-layouts  9.5 us (6%)
  matrix products  8.86 us (6%)
  other arithmetic  4.88 us (3%)
    pallas_call x1, Pallas kernels, exchange(): pl.pallas_call(exchange_kernel, out_shape=(jax.ShapeDtypeStruct((rows, wi...  127 us
    unnamed x23, local copies, waits for them, and re-layouts  6.85 us

profile of v3, /device:TPU:1, one launch (start us, length us, event | category | flops | bytes accessed | tf_op | source)
XLA Modules:
  0.0 151.3 jit_solution(9254578407895710128)
XLA Ops:
  0.6 0.0 copy-start.7
  0.6 2.6 %fusion.3 = bf16[128,2,2048]{2,0,1:T(8,128)(2,1)S(1)} fusion(bf16[128,2,2048]{2,1,0:T(2,128)(2,1)} %param.7, bf16[128,2,2048]{2,1,0:T(2,128)(2,1)} %param.6), kind=kLoop, calls=%fused_computation.15 | loop fusion | flops 4194304 | bytes 3145728 | tf_op jit(solution)/shard_map/convert_element_type | solution.py:487
  3.2 0.0 copy-done.7
  3.2 0.2 fusion.13
  3.5 0.1 iota_compare_fusion
  3.5 0.6 fusion.16
  4.1 0.0 copy-start.6
  4.1 1.7 %add_convert_fusion.hs = bf16[384,2048]{1,0:T(8,128)(2,1)} fusion(f32[384,2048]{1,0:T(8,128)S(1)} %fusion.16, bf16[128,2,2048]{2,0,1:T(8,128)(2,1)S(1)} %fusion.3, pred[384,256]{1,0:T(32,128)(4,1)S(1)} %iota_compare_fusion), kind=kOutput, calls=%fused_computation.4 | convolution fusion | flops 202899456 | bytes 5292032 | tf_op jit(solution)/shard_map/dot_general | solution.py:490
  5.8 0.0 copy-done.6
  5.8 1.1 constant_dynamic-slice_fusion.3
  6.9 0.5 fusion.18
  7.4 1.6 %fusion.gs = bf16[384,1536]{1,0:T(8,128)(2,1)} fusion(f32[384,1536]{1,0:T(8,128)S(1)} %fusion.18, f32[128]{0:T(128)S(1)} %get-tuple-element.31, pred[384,256]{1,0:T(32,128)(4,1)S(1)} %iota_compare_fusion, bf16[128,384]{1,0:T(8,128)(2,1)S(1)} %get-tuple-element.27, bf16[128,384]{1,0:T(8,128)(2,1)S(1)} %get-tuple-element.28, ...), kind=kOutput, calls=%fused_computation.6 | convolution fusion | flops 154140672 | bytes 3981824 | tf_op jit(solution)/shard_map/dot_general | solution.py:503
  9.0 127.2 %shard_map.101 = (bf16[384,1536]{1,0:T(8,128)(2,1)}, bf16[768,2048]{1,0:T(8,128)(2,1)}, bf16[2048,1536]{1,0:T(8,128)(2,1)}, f32[8,384]{1,0:T(8,128)}) custom-call(bf16[384,2048]{1,0:T(8,128)(2,1)} %add_convert_fusion.hs, bf16[384,1536]{1,0:T(8,128)(2,1)} %fusion.gs, bf16[2048,1536]{1,0:T(8,128)(2,1)} %bitcast.31), custom_call_target="tpu_custom_call" | custom-call | flops 28991029248 | bytes 30000000 | tf_op jit(solution)/shard_map/pallas_call | solution.py:429
  136.2 0.0 copy-start.1
  136.2 0.1 iota_compare_fusion.1
  136.3 0.0 copy-start.4
  136.4 1.8 %convolution_multiply_fusion.1 = f32[128,1536]{1,0:T(8,128)S(1)} fusion(bf16[384,1536]{1,0:T(8,128)(2,1)} %get-tuple-element.9, f32[128]{0:T(128)S(1)} %get-tuple-element.32, pred[256,384]{1,0:T(32,128)(4,1)S(1)} %iota_compare_fusion.1), kind=kOutput, calls=%fused_computation.11 | convolution fusion | flops 151191552 | bytes 2015744 | tf_op jit(solution)/shard_map/dot_general | solution.py:509
  138.1 0.0 copy-done.4
  138.2 0.0 copy-done.1
  138.2 0.0 copy-start
  138.2 0.4 fusion.2
  138.6 0.8 reshape.54
  139.4 0.7 slice_reduce_fusion
  140.1 0.2 select_reduce_fusion
  140.3 0.6 maximum_divide_fusion
  140.9 0.0 copy-done
  140.9 0.0 copy-start.5
  140.9 0.0 copy-start.2
  140.9 0.0 copy-start.3
  140.9 1.6 %convolution_bitcast_fusion = f32[128,1,2048]{2,0,1:T(8,128)S(1)} fusion(bf16[768,2048]{1,0:T(8,128)(2,1)S(1)} %copy-done, pred[256,384]{1,0:T(32,128)(4,1)} %copy-done.4), kind=kOutput, calls=%fused_computation.12 | convolution fusion | flops 402751488 | bytes 4292608 | tf_op jit(solution)/shard_map/dot_general | solution.py:518
  142.5 0.0 copy-done.5
  142.5 0.0 slice-start
  142.5 0.6 convolution_bitcast_fusion.1
  143.1 0.0 copy-done.2
  143.1 0.0 copy-done.3
  143.1 0.0 slice-start.1
  143.1 1.4 fusion.12
  144.5 2.0 %copy.17 = bf16[128,2,2048]{2,1,0:T(2,128)(2,1)} copy(bf16[128,2,2048]{2,0,1:T(8,128)(2,1)S(1)} %get-tuple-element.24) | data formatting | bytes 2097152
  146.5 2.0 %copy.18 = bf16[128,2,2048]{2,1,0:T(2,128)(2,1)} copy(bf16[128,2,2048]{2,0,1:T(8,128)(2,1)S(1)} %get-tuple-element.23) | data formatting | bytes 2097152
  148.6 0.0 slice-done
  148.6 0.0 slice-done.1
  148.6 2.7 %copy.29 = bf16[1,2048,1536]{2,1,0:T(8,128)(2,1)} copy(bf16[1,2048,1536]{2,1,0:T(8,128)(2,1)S(1)} %bitcast.30) | data formatting | bytes 12582912
  (6 shorter events, 0.0 us)
Async XLA Ops:
  0.6 2.6 %copy-start.7 = (s32[128,2]{0,1:T(2,128)S(1)}, s32[128,2]{0,1:T(2,128)}, u32[]{:S(2)}) copy-start(s32[128,2]{0,1:T(2,128)} %param.10) | copy-start | bytes 3076
  4.1 1.7 %copy-start.6 = (f32[128,2]{0,1:T(2,128)S(1)}, f32[128,2]{0,1:T(2,128)}, u32[]{:S(2)}) copy-start(f32[128,2]{0,1:T(2,128)} %param.9) | copy-start | bytes 3076
  136.2 1.9 %copy-start.1 = (bf16[384,1536]{1,0:T(8,128)(2,1)S(1)}, bf16[384,1536]{1,0:T(8,128)(2,1)}, u32[]{:S(2)}) copy-start(bf16[384,1536]{1,0:T(8,128)(2,1)} %get-tuple-element.9) | copy-start | bytes 3538948
  136.3 1.8 %copy-start.4 = (pred[256,384]{1,0:T(32,128)(4,1)}, pred[256,384]{1,0:T(32,128)(4,1)S(1)}, u32[]{:S(2)}) copy-start(pred[256,384]{1,0:T(32,128)(4,1)S(1)} %iota_compare_fusion.1) | copy-start | bytes 294916
  138.2 2.7 %copy-start = (bf16[768,2048]{1,0:T(8,128)(2,1)S(1)}, bf16[768,2048]{1,0:T(8,128)(2,1)}, u32[]{:S(2)}) copy-start(bf16[768,2048]{1,0:T(8,128)(2,1)} %get-tuple-element.11) | copy-start | bytes 9437188
  140.9 1.6 %copy-start.5 = (pred[256,384]{1,0:T(32,128)(4,1)S(1)}, pred[256,384]{1,0:T(32,128)(4,1)}, u32[]{:S(2)}) copy-start(pred[256,384]{1,0:T(32,128)(4,1)} %copy-done.4) | copy-start | bytes 294916
  140.9 2.2 %copy-start.2 = (bf16[128,2,2048]{2,1,0:T(2,128)(2,1)S(1)}, bf16[128,2,2048]{2,1,0:T(2,128)(2,1)}, u32[]{:S(2)}) copy-start(bf16[128,2,2048]{2,1,0:T(2,128)(2,1)} %param.7) | copy-start | bytes 3145732
  140.9 2.2 %copy-start.3 = (bf16[128,2,2048]{2,1,0:T(2,128)(2,1)S(1)}, bf16[128,2,2048]{2,1,0:T(2,128)(2,1)}, u32[]{:S(2)}) copy-start(bf16[128,2,2048]{2,1,0:T(2,128)(2,1)} %param.6) | copy-start | bytes 3145732
  142.5 6.1 %slice-start = ((s8[6291456]{0:T(1024)(128)(4,1)}), s8[4194304]{0:T(1024)(128)(4,1)S(1)}, s32[]{:S(2)}) async-start(s8[6291456]{0:T(1024)(128)(4,1)} %bitcast.28), calls=%async_computation | async-start | bytes 8388608
  143.1 5.5 %slice-start.1 = ((s8[6291456]{0:T(1024)(128)(4,1)}), s8[2097152]{0:T(1024)(128)(4,1)S(1)}, s32[]{:S(2)}) async-start(s8[6291456]{0:T(1024)(128)(4,1)} %bitcast.28), calls=%async_computation.1 | async-start | bytes 4194304

commit v4 on v3

--- a/solution.py
+++ b/solution.py
@@ -14,11 +14,11 @@
 
 
 def exchange_kernel(
-    hs, gs, w_hbm, oh, bh, wg, cg,
-    w, hr, gr, os, opx, orx, od, bs, br, wt, cgs, cgr,
+    pack, unpack, h0, h1, comb, grad_hbm, w_hbm, mixed, hg, wg, cg,
+    mine, hs, gs, oh, bh, w, hr, gr, os, opx, orx, od, bs, br, wt, cgs, cgr,
     send_h, send_g, recv_h, recv_g, xg_send, xg_recv, xf_send, xf_recv, sib_send, sib_recv,
     xp_send, xp_recv, xo_send, xo_recv, bsib_send, bsib_recv, home_o_send, home_b_send,
-    home_recv, wg_sem, w_sem, cg_send, cg_recv,
+    home_recv, wg_sem, w_sem, mine_sem, cg_send, cg_recv,
 ):
     me = lax.axis_index("dp")
     x = lax.axis_index("hid")
@@ -35,6 +35,14 @@
     def m(v, k):
         return pl.multiple_of(v, k)
 
+    def mine_copy(j):
+        cols = pl.ds(m(j * 4 * q_w + x * q_w, 128), q_w)
+        return pltpu.make_async_copy(
+            grad_hbm.at[:, cols], mine.at[:, j * q_w : (j + 1) * q_w], mine_sem.at[j]
+        )
+
+    for j in range(4):
+        mine_copy(j).start()
     w_copy = pltpu.make_async_copy(w_hbm, w, w_sem)
     w_copy.start()
 
@@ -50,6 +58,18 @@
         pl.semaphore_signal(
             barrier, inc=1, device_id=(me, lax.rem(x + o, 4)), device_id_type=MESH
         )
+
+    tokens = mine.shape[0]
+    for j in range(4):
+        mine_copy(j).wait()
+        cols = slice(j * q_w, (j + 1) * q_w)
+        part = mine[:, cols].astype(F32)
+        rows = jnp.dot(
+            pack[:, :tokens], (comb[:, 0:1] * part).astype(BF16), preferred_element_type=F32
+        ) + jnp.dot(
+            pack[:, tokens:], (comb[:, 1:2] * part).astype(BF16), preferred_element_type=F32
+        )
+        gs[:, cols] = rows.astype(BF16)
     pl.semaphore_wait(barrier, 34)
 
     my_half = m(core * half_w, 128)
@@ -76,11 +96,6 @@
         gs.at[pl.ds(my_expert_rows, CAP), pl.ds(m(j_me * q_w, 128), q_w)],
         gr.at[slot_rows(0, core), pl.ds(my_quarter, q_w)],
         recv_g.at[0],
-    ).start()
-    pltpu.make_async_copy(
-        hs.at[pl.ds(my_expert_rows, CAP), pl.ds(my_half, half_w)],
-        hr.at[slot_rows(0, core), pl.ds(my_half, half_w)],
-        recv_h.at[0],
     ).start()
 
     def g_copy(n):
@@ -115,15 +130,22 @@
 
         lax.fori_loop(lo, hi, step, 0)
 
-    loop(1, 16, lambda n: g_copy(n).start())
-    loop(1, 8, lambda n: h_copy(n).start())
-
-    def issue(r):
-        loop(r * 8, r * 8 + 8, lambda n: g_copy(n).start())
-        loop(r * 8 - 8, r * 8, lambda n: h_copy(n).start())
-
-    loop(2, 4, issue)
-    loop(24, 32, lambda n: h_copy(n).start())
+    loop(1, 32, lambda n: g_copy(n).start())
+
+    def pack_h(n):
+        cols = pl.ds(m(n * 512, 128), 512)
+        rows = jnp.dot(pack[:, :tokens], h0[:, cols], preferred_element_type=F32) + jnp.dot(
+            pack[:, tokens:], h1[:, cols], preferred_element_type=F32
+        )
+        hs[:, cols] = rows.astype(BF16)
+
+    loop(0, hr.shape[1] // 512, pack_h)
+    pltpu.make_async_copy(
+        hs.at[pl.ds(my_expert_rows, CAP), pl.ds(my_half, half_w)],
+        hr.at[slot_rows(0, core), pl.ds(my_half, half_w)],
+        recv_h.at[0],
+    ).start()
+    loop(1, 32, lambda n: h_copy(n).start())
 
     half_rows = rows_n // 2
 
@@ -370,17 +392,29 @@
     loop(0, 6, step)
 
     pltpu.make_async_copy(oh, oh, home_recv.at[0]).wait()
-    fold = jnp.zeros((rows_n, 128), F32)
-    for k in range(4 * q_w // 128):
-        cols = slice(k * 128, (k + 1) * 128)
-        fold = fold + oh[:, cols].astype(F32) * gs[:, cols].astype(F32)
-    high = fold.astype(BF16)
-    low = (fold - high.astype(F32)).astype(BF16)
     ones = jnp.ones((8, 128), BF16)
     last = (((1,), (1,)), ((), ()))
-    cgs[...] = lax.dot_general(ones, high, last, preferred_element_type=F32) + lax.dot_general(
-        ones, low, last, preferred_element_type=F32
-    )
+    folds = [jnp.zeros((tokens, 128), F32), jnp.zeros((tokens, 128), F32)]
+    for j in range(4):
+        cols = slice(j * q_w, (j + 1) * q_w)
+        part = mine[:, cols].astype(F32)
+        total = None
+        for t in range(2):
+            slot_out = jnp.dot(
+                unpack[t * tokens : (t + 1) * tokens, :], oh[:, cols], preferred_element_type=F32
+            )
+            term = comb[:, t : t + 1] * slot_out
+            total = term if total is None else total + term
+            terms = part * slot_out
+            for k in range(q_w // 128):
+                folds[t] = folds[t] + terms[:, k * 128 : (k + 1) * 128]
+        mixed[:, cols] = total.astype(BF16)
+    for t in range(2):
+        high = folds[t].astype(BF16)
+        low = (folds[t] - high.astype(F32)).astype(BF16)
+        cgs[:, t * tokens : (t + 1) * tokens] = lax.dot_general(
+            ones, high, last, preferred_element_type=F32
+        ) + lax.dot_general(ones, low, last, preferred_element_type=F32)
 
     def cg_copy(o):
         return pltpu.make_async_remote_copy(
@@ -391,11 +425,20 @@
 
     for o in range(1, 4):
         cg_copy(o).start()
+
+    pltpu.make_async_copy(bh, bh, home_recv.at[1]).wait()
+
+    def unpack_b(n):
+        cols = pl.ds(m(n * 512, 128), 512)
+        hg[:, cols] = jnp.dot(
+            unpack[...], bh[:rows_n, cols], preferred_element_type=F32
+        ) + jnp.dot(unpack[...], bh[rows_n:, cols], preferred_element_type=F32)
+
+    loop(0, hr.shape[1] // 512, unpack_b)
     for o in range(1, 4):
         cg_copy(o).wait_recv()
     cg[...] = cgs[...] + cgr[0] + cgr[1] + cgr[2]
 
-    pltpu.make_async_copy(bh, bh, home_recv.at[1]).wait()
     for o in range(1, 4):
         cg_copy(o).wait_send()
     loop(0, 8, lambda n: wg_copy(n).wait())
@@ -420,23 +463,30 @@
     loop(0, 4, drain_r)
 
 
-def exchange(hs, gs, w):
-    rows, ff = hs.shape
-    width = gs.shape[1]
+def exchange(pack, unpack, h0, h1, comb, grad, w):
+    rows = pack.shape[0]
+    tokens, ff = h0.shape
+    width = w.shape[1]
     rows_all = 32 * CAP
     vmem = pl.BlockSpec(memory_space=pltpu.VMEM)
+    hbm = pl.BlockSpec(memory_space=pl.ANY)
     dma = pltpu.SemaphoreType.DMA
     return pl.pallas_call(
         exchange_kernel,
         out_shape=(
-            jax.ShapeDtypeStruct((rows, width), BF16),
-            jax.ShapeDtypeStruct((2 * rows, ff), BF16),
+            jax.ShapeDtypeStruct((tokens, width), BF16),
+            jax.ShapeDtypeStruct((2 * tokens, ff), F32),
             jax.ShapeDtypeStruct((ff, width), BF16),
-            jax.ShapeDtypeStruct((8, rows), F32),
+            jax.ShapeDtypeStruct((8, 2 * tokens), F32),
         ),
-        in_specs=[vmem, vmem, pl.BlockSpec(memory_space=pl.ANY)],
-        out_specs=(vmem, vmem, pl.BlockSpec(memory_space=pl.ANY), vmem),
+        in_specs=[vmem, vmem, vmem, vmem, vmem, hbm, hbm],
+        out_specs=(vmem, vmem, hbm, vmem),
         scratch_shapes=[
+            pltpu.VMEM((tokens, width), BF16),
+            pltpu.VMEM((rows, ff), BF16),
+            pltpu.VMEM((rows, width), BF16),
+            pltpu.VMEM((rows, width), BF16),
+            pltpu.VMEM((2 * rows, ff), BF16),
             pltpu.VMEM((ff, width), BF16),
             pltpu.VMEM((rows_all, ff), BF16),
             pltpu.VMEM((rows_all, width), BF16),
@@ -447,12 +497,12 @@
             pltpu.VMEM((rows_all, ff), BF16),
             pltpu.VMEM((rows_all, ff // 2), BF16),
             pltpu.VMEM((ff, width), BF16),
-            pltpu.VMEM((8, rows), F32),
-            pltpu.VMEM((3, 8, rows), F32),
+            pltpu.VMEM((8, 2 * tokens), F32),
+            pltpu.VMEM((3, 8, 2 * tokens), F32),
             dma((32,)), dma((32,)), dma((4,)), dma((4,)),
             dma((4, 2)), dma((4, 2)), dma((4, 2)), dma((4, 2)), dma((4,)), dma((4,)),
             dma((4, 2)), dma((4, 2)), dma((4, 2)), dma((4, 2)), dma((4,)), dma((4,)),
-            dma((32,)), dma((32,)), dma((2,)), dma((8,)), dma, dma((3,)), dma((3,)),
+            dma((32,)), dma((32,)), dma((2,)), dma((8,)), dma, dma((4,)), dma((3,)), dma((3,)),
         ],
         compiler_params=pltpu.CompilerParams(
             collective_id=0, has_side_effects=True, vmem_limit_bytes=62 * 1024 * 1024
@@ -460,14 +510,12 @@
         cost_estimate=pl.CostEstimate(
             flops=6 * rows_all * ff * width, bytes_accessed=30000000, transcendentals=0
         ),
-    )(hs, gs, w)
+    )(pack, unpack, h0, h1, comb, grad, w)
 
 
 def per_device(gate_pre, up_pre, out_grad, combine, expert_ids, down_weight):
     tokens = gate_pre.shape[0]
-    x = lax.axis_index("hid")
     width = down_weight.shape[2]
-    quarter = width // 4
     rows = E * CAP
     flat = jnp.concatenate([expert_ids[:, 0], expert_ids[:, 1]])
     onehot = (flat[:, None] == jnp.arange(E, dtype=jnp.int32)[None, :]).astype(BF16)
@@ -478,47 +526,18 @@
     target = flat * CAP + position
     row_ids = jnp.arange(rows, dtype=jnp.int32)
     pack = (target[None, :] == row_ids[:, None]).astype(BF16)
-    hit = target[:, None] == row_ids[None, :]
-    unpack = hit.astype(BF16)
+    unpack = (target[:, None] == row_ids[None, :]).astype(BF16)
 
     gate_f = gate_pre.astype(F32)
     up_f = up_pre.astype(F32)
     sig = jax.nn.sigmoid(gate_f)
     hidden = (gate_f * sig * up_f).astype(BF16)
-    hs = (
-        jnp.dot(pack[:, :tokens], hidden[:, 0], preferred_element_type=F32)
-        + jnp.dot(pack[:, tokens:], hidden[:, 1], preferred_element_type=F32)
-    ).astype(BF16)
-    mine = jnp.concatenate(
-        [
-            lax.dynamic_slice_in_dim(out_grad, j * width + x * quarter, quarter, axis=1)
-            for j in range(4)
-        ],
-        axis=1,
-    ).astype(F32)
-    scaled0 = (combine[:, 0:1] * mine).astype(BF16)
-    scaled1 = (combine[:, 1:2] * mine).astype(BF16)
-    gs = (
-        jnp.dot(pack[:, :tokens], scaled0, preferred_element_type=F32)
-        + jnp.dot(pack[:, tokens:], scaled1, preferred_element_type=F32)
-    ).astype(BF16)
-
-    oh, bh, wg, cg = exchange(hs, gs, down_weight[0])
-
-    mixed = (
-        combine[:, 0:1] * jnp.dot(unpack[:tokens], oh, preferred_element_type=F32)
-        + combine[:, 1:2] * jnp.dot(unpack[tokens:], oh, preferred_element_type=F32)
-    ).astype(BF16).reshape(tokens, 4, quarter)
-    slot_cg = jnp.sum(jnp.where(hit, cg[0:1, :], 0.0), axis=1)
-    combine_grad = jnp.stack([slot_cg[:tokens], slot_cg[tokens:]], axis=1) / combine
-    both = jnp.concatenate([unpack, unpack], axis=1)
-    hidden_grad = jnp.stack(
-        [
-            jnp.dot(both[:tokens], bh, preferred_element_type=F32),
-            jnp.dot(both[tokens:], bh, preferred_element_type=F32),
-        ],
-        axis=1,
+    mixed, hg, wg, cg = exchange(
+        pack, unpack, hidden[:, 0], hidden[:, 1], combine, out_grad, down_weight[0]
     )
+    mixed = mixed.reshape(tokens, 4, width // 4)
+    combine_grad = jnp.stack([cg[0, :tokens], cg[0, tokens:]], axis=1)
+    hidden_grad = jnp.stack([hg[:tokens], hg[tokens:]], axis=1)
     gate_grad = (hidden_grad * up_f * sig * (1.0 + gate_f * (1.0 - sig))).astype(BF16)
     up_grad = (hidden_grad * gate_f * sig).astype(BF16)
     return mixed, combine_grad, gate_grad, up_grad, wg[None]

time: 152 us -> 144 us (0.947)
  matrix products: 8.86 us -> 0.19 us
  Pallas kernels: 127 us -> 122 us
  local copies, waits for them, and re-layouts: 9.5 us -> 14.5 us
    dot_general x8 -> x0, matrix products: 8.66 us -> none  [the longest x1 1.78 us: per_device(): jnp.dot(unpack[:tokens], oh, preferred_element_type=F32)]
    pallas_call x1, Pallas kernels: 127 us -> 122 us  [exchange(): pl.pallas_call(exchange_kernel, out_shape=(jax.ShapeDtypeStruct((tokens,...]
    another operation x1 -> x2, local copies, waits for them, and re-layouts: 0.01 us -> 2.52 us  [the longest x1 1.83 us: per_device(): hidden_grad = jnp.stack([hg[:tokens], hg[tokens:]], axis=1)]
    unnamed x23 -> x12, local copies, waits for them, and re-layouts: 6.85 us -> 8.22 us
where the time goes in v4:
time: 144 us; the launch traced here: 143 us
  Pallas kernels  122 us (85%)
  local copies, waits for them, and re-layouts  14.5 us (10%)
  other arithmetic  6.01 us (4%)
    pallas_call x1, Pallas kernels, exchange(): pl.pallas_call(exchange_kernel, out_shape=(jax.ShapeDtypeStruct((tokens,...  122 us
    unnamed x12, local copies, waits for them, and re-layouts  8.22 us

profile of v4, /device:TPU:1, one launch (start us, length us, event | category | flops | bytes accessed | tf_op | source)
XLA Modules:
  0.0 143.4 jit_solution(9604774689226305498)
XLA Ops:
  0.6 0.8 slice_bitcast_fusion.7
  1.4 0.2 fusion.10
  1.6 1.4 copy.13.comb
  3.0 0.8 fusion.12.unpack
  3.8 0.7 fusion.11.pack
  4.5 2.6 %fusion = bf16[128,2,2048]{2,0,1:T(8,128)(2,1)S(1)} fusion(bf16[128,2,2048]{2,1,0:T(2,128)(2,1)} %param.7, bf16[128,2,2048]{2,1,0:T(2,128)(2,1)} %param.6), kind=kLoop, calls=%fused_computation.6 | loop fusion | flops 4194304 | bytes 3145728 | tf_op jit(solution)/shard_map/convert_element_type | solution.py:534
  7.1 1.0 slice_bitcast_fusion.2
  8.1 0.0 copy-start
  8.1 122.1 %shard_map.101 = (bf16[128,1536]{1,0:T(8,128)(2,1)}, f32[256,2048]{1,0:T(8,128)}, bf16[2048,1536]{1,0:T(8,128)(2,1)}, f32[8,256]{1,0:T(8,128)}) custom-call(bf16[384,256]{1,0:T(8,128)(2,1)} %fusion.11.pack, bf16[256,384]{1,0:T(8,128)(2,1)} %fusion.12.unpack, bf16[128,2048]{1,0:T(8,128)(2,1)} %get-tuple-element.23.h0, ...), custom_call_target="tpu_custom_call" | custom-call | flops 28991029248 | bytes 30000000 | tf_op jit(solution)/shard_map/pallas_call | solution.py:474
  130.2 0.0 copy-start.1
  130.2 1.9 %reshape.54 = bf16[128,4,384]{2,1,0:T(4,128)(2,1)} reshape(bf16[128,1536]{1,0:T(8,128)(2,1)} %get-tuple-element.9) | data formatting | bytes 786432 | tf_op jit(solution)/shard_map/reshape | solution.py:538
  132.1 0.7 slice_bitcast_fusion.5
  132.8 0.6 pad_maximum_fusion.1
  133.4 0.0 slice-start
  133.4 1.8 %slice_bitcast_fusion.1 = (f32[128,1,2048]{2,0,1:T(8,128)S(1)}, f32[128,1,2048]{2,0,1:T(8,128)S(1)}) fusion(f32[256,2048]{1,0:T(8,128)} %get-tuple-element.11), kind=kLoop, calls=%fused_computation.20 | loop fusion | bytes 4194304 | tf_op jit(solution)/shard_map/stack | solution.py:540
  135.2 0.0 copy-done
  135.2 0.0 copy-done.1
  135.3 0.0 slice-start.1
  135.3 1.4 fusion.9
  136.6 2.0 %copy.15 = bf16[128,2,2048]{2,1,0:T(2,128)(2,1)} copy(bf16[128,2,2048]{2,0,1:T(8,128)(2,1)S(1)} %get-tuple-element.18) | data formatting | bytes 2097152
  138.7 2.0 %copy.14 = bf16[128,2,2048]{2,1,0:T(2,128)(2,1)} copy(bf16[128,2,2048]{2,0,1:T(8,128)(2,1)S(1)} %get-tuple-element.19) | data formatting | bytes 2097152
  140.7 0.0 slice-done
  140.7 0.0 slice-done.1
  140.7 2.7 %copy.22 = bf16[1,2048,1536]{2,1,0:T(8,128)(2,1)} copy(bf16[1,2048,1536]{2,1,0:T(8,128)(2,1)S(1)} %bitcast.20) | data formatting | bytes 12582912
  (3 shorter events, 0.0 us)
Async XLA Ops:
  8.1 127.1 %copy-start = (bf16[128,2,2048]{2,1,0:T(2,128)(2,1)S(1)}, bf16[128,2,2048]{2,1,0:T(2,128)(2,1)}, u32[]{:S(2)}) copy-start(bf16[128,2,2048]{2,1,0:T(2,128)(2,1)} %param.7) | copy-start | bytes 3145732
  130.2 5.1 %copy-start.1 = (bf16[128,2,2048]{2,1,0:T(2,128)(2,1)S(1)}, bf16[128,2,2048]{2,1,0:T(2,128)(2,1)}, u32[]{:S(2)}) copy-start(bf16[128,2,2048]{2,1,0:T(2,128)(2,1)} %param.6) | copy-start | bytes 3145732
  133.4 7.3 %slice-start = ((s8[6291456]{0:T(1024)(128)(4,1)}), s8[4194304]{0:T(1024)(128)(4,1)S(1)}, s32[]{:S(2)}) async-start(s8[6291456]{0:T(1024)(128)(4,1)} %bitcast.18), calls=%async_computation | async-start | bytes 8388608
  135.3 5.5 %slice-start.1 = ((s8[6291456]{0:T(1024)(128)(4,1)}), s8[2097152]{0:T(1024)(128)(4,1)S(1)}, s32[]{:S(2)}) async-start(s8[6291456]{0:T(1024)(128)(4,1)} %bitcast.18), calls=%async_computation.1 | async-start | bytes 4194304

commit v5 on v4

--- a/solution.py
+++ b/solution.py
@@ -14,8 +14,8 @@
 
 
 def exchange_kernel(
-    pack, unpack, h0, h1, comb, grad_hbm, w_hbm, mixed, hg, wg, cg,
-    mine, hs, gs, oh, bh, w, hr, gr, os, opx, orx, od, bs, br, wt, cgs, cgr,
+    slot_row, hidden, comb, grad_hbm, w_hbm, mixed, hg, wg, cg,
+    pack, mine, hs, gs, oh, bh, w, hr, gr, os, opx, orx, od, bs, br, wt, cgs, cgr,
     send_h, send_g, recv_h, recv_g, xg_send, xg_recv, xf_send, xf_recv, sib_send, sib_recv,
     xp_send, xp_recv, xo_send, xo_recv, bsib_send, bsib_recv, home_o_send, home_b_send,
     home_recv, wg_sem, w_sem, mine_sem, cg_send, cg_recv,
@@ -60,14 +60,24 @@
         )
 
     tokens = mine.shape[0]
+    row_ids = lax.broadcasted_iota(jnp.int32, pack.shape, 0)
+    pack[...] = (slot_row[...] == row_ids).astype(F32).astype(BF16)
+    diagonal = lax.broadcasted_iota(jnp.int32, (tokens, tokens), 0) == lax.broadcasted_iota(
+        jnp.int32, (tokens, tokens), 1
+    )
+
+    def weight_of(t):
+        return jnp.sum(jnp.where(diagonal, comb[t : t + 1, :], 0.0), axis=1, keepdims=True)
+
+    combine = [weight_of(0), weight_of(1)]
     for j in range(4):
         mine_copy(j).wait()
         cols = slice(j * q_w, (j + 1) * q_w)
         part = mine[:, cols].astype(F32)
         rows = jnp.dot(
-            pack[:, :tokens], (comb[:, 0:1] * part).astype(BF16), preferred_element_type=F32
+            pack[:, :tokens], (combine[0] * part).astype(BF16), preferred_element_type=F32
         ) + jnp.dot(
-            pack[:, tokens:], (comb[:, 1:2] * part).astype(BF16), preferred_element_type=F32
+            pack[:, tokens:], (combine[1] * part).astype(BF16), preferred_element_type=F32
         )
         gs[:, cols] = rows.astype(BF16)
     pl.semaphore_wait(barrier, 34)
@@ -134,8 +144,8 @@
 
     def pack_h(n):
         cols = pl.ds(m(n * 512, 128), 512)
-        rows = jnp.dot(pack[:, :tokens], h0[:, cols], preferred_element_type=F32) + jnp.dot(
-            pack[:, tokens:], h1[:, cols], preferred_element_type=F32
+        rows = jnp.dot(pack[:, :tokens], hidden[0, :, cols], preferred_element_type=F32) + jnp.dot(
+            pack[:, tokens:], hidden[1, :, cols], preferred_element_type=F32
         )
         hs[:, cols] = rows.astype(BF16)
 
@@ -392,6 +402,12 @@
     loop(0, 6, step)
 
     pltpu.make_async_copy(oh, oh, home_recv.at[0]).wait()
+    def unpack(t, rows):
+        return lax.dot_general(
+            pack[:, t * tokens : (t + 1) * tokens], rows, (((0,), (0,)), ((), ())),
+            preferred_element_type=F32,
+        )
+
     ones = jnp.ones((8, 128), BF16)
     last = (((1,), (1,)), ((), ()))
     folds = [jnp.zeros((tokens, 128), F32), jnp.zeros((tokens, 128), F32)]
@@ -400,19 +416,17 @@
         part = mine[:, cols].astype(F32)
         total = None
         for t in range(2):
-            slot_out = jnp.dot(
-                unpack[t * tokens : (t + 1) * tokens, :], oh[:, cols], preferred_element_type=F32
-            )
-            term = comb[:, t : t + 1] * slot_out
+            slot_out = unpack(t, oh[:, cols])
+            term = combine[t] * slot_out
             total = term if total is None else total + term
             terms = part * slot_out
             for k in range(q_w // 128):
                 folds[t] = folds[t] + terms[:, k * 128 : (k + 1) * 128]
-        mixed[:, cols] = total.astype(BF16)
+        mixed[j] = total.astype(BF16)
     for t in range(2):
         high = folds[t].astype(BF16)
         low = (folds[t] - high.astype(F32)).astype(BF16)
-        cgs[:, t * tokens : (t + 1) * tokens] = lax.dot_general(
+        cgs[t * 8 : (t + 1) * 8, :] = lax.dot_general(
             ones, high, last, preferred_element_type=F32
         ) + lax.dot_general(ones, low, last, preferred_element_type=F32)
 
@@ -430,14 +444,15 @@
 
     def unpack_b(n):
         cols = pl.ds(m(n * 512, 128), 512)
-        hg[:, cols] = jnp.dot(
-            unpack[...], bh[:rows_n, cols], preferred_element_type=F32
-        ) + jnp.dot(unpack[...], bh[rows_n:, cols], preferred_element_type=F32)
+        for t in range(2):
+            hg[t, :, cols] = unpack(t, bh[:rows_n, cols]) + unpack(t, bh[rows_n:, cols])
 
     loop(0, hr.shape[1] // 512, unpack_b)
     for o in range(1, 4):
         cg_copy(o).wait_recv()
-    cg[...] = cgs[...] + cgr[0] + cgr[1] + cgr[2]
+    total = cgs[...] + cgr[0] + cgr[1] + cgr[2]
+    cg[0:1, :] = total[0:1, :]
+    cg[1:2, :] = total[8:9, :]
 
     for o in range(1, 4):
         cg_copy(o).wait_send()
@@ -463,9 +478,9 @@
     loop(0, 4, drain_r)
 
 
-def exchange(pack, unpack, h0, h1, comb, grad, w):
-    rows = pack.shape[0]
-    tokens, ff = h0.shape
+def exchange(slot_row, hidden, comb, grad, w):
+    rows = E * CAP
+    _, tokens, ff = hidden.shape
     width = w.shape[1]
     rows_all = 32 * CAP
     vmem = pl.BlockSpec(memory_space=pltpu.VMEM)
@@ -474,14 +489,15 @@
     return pl.pallas_call(
         exchange_kernel,
         out_shape=(
-            jax.ShapeDtypeStruct((tokens, width), BF16),
-            jax.ShapeDtypeStruct((2 * tokens, ff), F32),
+            jax.ShapeDtypeStruct((4, tokens, width // 4), BF16),
+            jax.ShapeDtypeStruct((2, tokens, ff), F32),
             jax.ShapeDtypeStruct((ff, width), BF16),
-            jax.ShapeDtypeStruct((8, 2 * tokens), F32),
+            jax.ShapeDtypeStruct((2, tokens), F32),
         ),
-        in_specs=[vmem, vmem, vmem, vmem, vmem, hbm, hbm],
+        in_specs=[vmem, vmem, vmem, hbm, hbm],
         out_specs=(vmem, vmem, hbm, vmem),
         scratch_shapes=[
+            pltpu.VMEM((rows, 2 * tokens), BF16),
             pltpu.VMEM((tokens, width), BF16),
             pltpu.VMEM((rows, ff), BF16),
             pltpu.VMEM((rows, width), BF16),
@@ -497,8 +513,8 @@
             pltpu.VMEM((rows_all, ff), BF16),
             pltpu.VMEM((rows_all, ff // 2), BF16),
             pltpu.VMEM((ff, width), BF16),
-            pltpu.VMEM((8, 2 * tokens), F32),
-            pltpu.VMEM((3, 8, 2 * tokens), F32),
+            pltpu.VMEM((16, tokens), F32),
+            pltpu.VMEM((3, 16, tokens), F32),
             dma((32,)), dma((32,)), dma((4,)), dma((4,)),
             dma((4, 2)), dma((4, 2)), dma((4, 2)), dma((4, 2)), dma((4,)), dma((4,)),
             dma((4, 2)), dma((4, 2)), dma((4, 2)), dma((4, 2)), dma((4,)), dma((4,)),
@@ -510,34 +526,30 @@
         cost_estimate=pl.CostEstimate(
             flops=6 * rows_all * ff * width, bytes_accessed=30000000, transcendentals=0
         ),
-    )(pack, unpack, h0, h1, comb, grad, w)
+    )(slot_row, hidden, comb, grad, w)
 
 
 def per_device(gate_pre, up_pre, out_grad, combine, expert_ids, down_weight):
     tokens = gate_pre.shape[0]
     width = down_weight.shape[2]
-    rows = E * CAP
     flat = jnp.concatenate([expert_ids[:, 0], expert_ids[:, 1]])
     onehot = (flat[:, None] == jnp.arange(E, dtype=jnp.int32)[None, :]).astype(BF16)
     count = tokens * TOP
     before = (jnp.arange(count)[:, None] > jnp.arange(count)[None, :]).astype(BF16)
     earlier = jnp.dot(before, onehot, preferred_element_type=F32)
     position = jnp.sum(earlier * onehot.astype(F32), axis=1).astype(jnp.int32)
-    target = flat * CAP + position
-    row_ids = jnp.arange(rows, dtype=jnp.int32)
-    pack = (target[None, :] == row_ids[:, None]).astype(BF16)
-    unpack = (target[:, None] == row_ids[None, :]).astype(BF16)
+    slot_row = (flat * CAP + position).reshape(1, count)
 
     gate_f = gate_pre.astype(F32)
     up_f = up_pre.astype(F32)
     sig = jax.nn.sigmoid(gate_f)
     hidden = (gate_f * sig * up_f).astype(BF16)
     mixed, hg, wg, cg = exchange(
-        pack, unpack, hidden[:, 0], hidden[:, 1], combine, out_grad, down_weight[0]
+        slot_row, jnp.transpose(hidden, (1, 0, 2)), combine.T, out_grad, down_weight[0]
     )
-    mixed = mixed.reshape(tokens, 4, width // 4)
-    combine_grad = jnp.stack([cg[0, :tokens], cg[0, tokens:]], axis=1)
-    hidden_grad = jnp.stack([hg[:tokens], hg[tokens:]], axis=1)
+    mixed = jnp.transpose(mixed, (1, 0, 2))
+    combine_grad = cg.T
+    hidden_grad = jnp.transpose(hg, (1, 0, 2))
     gate_grad = (hidden_grad * up_f * sig * (1.0 + gate_f * (1.0 - sig))).astype(BF16)
     up_grad = (hidden_grad * gate_f * sig).astype(BF16)
     return mixed, combine_grad, gate_grad, up_grad, wg[None]

time: 144 us -> 141 us (0.979)
  local copies, waits for them, and re-layouts: 14.5 us -> 10.2 us
    convert_element_type x3 -> x1, other arithmetic: 4.06 us -> 0.01 us  [per_device(): position = jnp.sum(earlier * onehot.astype(F32), axis=1).astype(jnp.int32)]
    transpose x0 -> x1, other arithmetic: none -> 3.52 us  [per_device(): jnp.transpose(hidden, (1, 0, 2))]
    another operation x2 -> x0, local copies, waits for them, and re-layouts: 2.52 us -> none  [the longest x1 1.83 us: per_device(): hidden_grad = jnp.stack([hg[:tokens], hg[tokens:]], axis=1)]
    convert_element_type x1, other arithmetic: 1.36 us -> 3.31 us  [per_device(): up_grad = (hidden_grad * gate_f * sig).astype(BF16)]
    reshape x1 -> x0, local copies, waits for them, and re-layouts: 1.92 us -> none  [per_device(): mixed = mixed.reshape(tokens, 4, width // 4)]
    unnamed x12 -> x11, local copies, waits for them, and re-layouts: 8.22 us -> 9.42 us
where the time goes in v5:
time: 141 us; the launch traced here: 140 us
  Pallas kernels  122 us (87%)
  local copies, waits for them, and re-layouts  10.2 us (7%)
  other arithmetic  7.41 us (5%)
    pallas_call x1, Pallas kernels, exchange(): pl.pallas_call(exchange_kernel, out_shape=(jax.ShapeDtypeStruct((4, token...  122 us
    unnamed x11, local copies, waits for them, and re-layouts  9.42 us
    transpose x1, other arithmetic, per_device(): jnp.transpose(hidden, (1, 0, 2))  3.52 us
    convert_element_type x1, other arithmetic, per_device(): up_grad = (hidden_grad * gate_f * sig).astype(BF16)  3.31 us

profile of v5, /device:TPU:1, one launch (start us, length us, event | category | flops | bytes accessed | tf_op | source)
XLA Modules:
  0.0 140.4 jit_solution(4632715619726771131)
XLA Ops:
  0.6 0.8 slice_bitcast_fusion.3
  1.4 0.2 fusion.10
  1.6 0.6 fusion.14.slot_row
  2.2 3.5 %fusion.11.hidden = bf16[2,128,2048]{2,1,0:T(8,128)(2,1)} fusion(bf16[128,2,2048]{2,1,0:T(2,128)(2,1)} %param.7, bf16[128,2,2048]{2,1,0:T(2,128)(2,1)} %param.6), kind=kLoop, calls=%fused_computation.18 | loop fusion | flops 4194304 | bytes 3145728 | tf_op jit(solution)/shard_map/transpose | solution.py:548
  5.7 0.0 copy-start.1
  5.7 122.0 %shard_map.101 = (bf16[4,128,384]{2,1,0:T(8,128)(2,1)}, f32[2,128,2048]{2,1,0:T(8,128)}, bf16[2048,1536]{1,0:T(8,128)(2,1)}, f32[2,128]{1,0:T(2,128)}) custom-call(s32[1,256]{1,0:T(1,128)} %fusion.14.slot_row, bf16[2,128,2048]{2,1,0:T(8,128)(2,1)} %fusion.11.hidden, f32[2,128]{1,0:T(2,128)} %bitcast.24, bf16[128,6144]{1,0:T(8,128)(2,1)} %grad_hbm.1, ...), custom_call_target="tpu_custom_call" | custom-call | flops 28991029248 | bytes 30000000 | tf_op jit(solution)/shard_map/pallas_call | solution.py:489
  127.7 2.0 %copy.13 = bf16[128,4,384]{2,1,0:T(4,128)(2,1)} copy(bf16[128,4,384]{2,0,1:T(8,128)(2,1)} %bitcast.20) | data formatting | bytes 786432
  129.7 0.0 copy-done.1
  129.7 0.0 copy-start
  129.7 3.3 %fusion.9 = (bf16[128,2,2048]{2,0,1:T(8,128)(2,1)S(1)}, bf16[128,2,2048]{2,0,1:T(8,128)(2,1)S(1)}) fusion(f32[2,128,2048]{2,1,0:T(8,128)} %get-tuple-element.11, bf16[128,2,2048]{2,1,0:T(2,128)(2,1)} %param.6, bf16[128,2,2048]{2,1,0:T(2,128)(2,1)S(1)} %copy-done.1), kind=kLoop, calls=%fused_computation.15 | loop fusion | flops 7864320 | bytes 6291456 | tf_op jit(solution)/shard_map/convert_element_type | solution.py:554
  133.0 0.0 copy-start.2
  133.1 2.0 %copy.15 = bf16[128,2,2048]{2,1,0:T(2,128)(2,1)} copy(bf16[128,2,2048]{2,0,1:T(8,128)(2,1)S(1)} %get-tuple-element.18) | data formatting | bytes 2097152
  135.1 2.0 %copy.14 = bf16[128,2,2048]{2,1,0:T(2,128)(2,1)} copy(bf16[128,2,2048]{2,0,1:T(8,128)(2,1)S(1)} %get-tuple-element.19) | data formatting | bytes 2097152
  137.2 0.0 copy-done.2
  137.2 0.6 copy.23
  137.7 0.0 copy-done
  137.7 2.7 %copy.24 = bf16[1,2048,1536]{2,1,0:T(8,128)(2,1)} copy(bf16[1,2048,1536]{2,1,0:T(8,128)(2,1)S(1)} %bitcast.19) | data formatting | bytes 12582912
  (2 shorter events, 0.0 us)
Async XLA Ops:
  5.7 124.0 %copy-start.1 = (bf16[128,2,2048]{2,1,0:T(2,128)(2,1)S(1)}, bf16[128,2,2048]{2,1,0:T(2,128)(2,1)}, u32[]{:S(2)}) copy-start(bf16[128,2,2048]{2,1,0:T(2,128)(2,1)} %param.7) | copy-start | bytes 3145732
  129.7 8.0 %copy-start = (bf16[2048,1536]{1,0:T(8,128)(2,1)S(1)}, bf16[2048,1536]{1,0:T(8,128)(2,1)}, u32[]{:S(2)}) copy-start(bf16[2048,1536]{1,0:T(8,128)(2,1)} %get-tuple-element.12) | copy-start | bytes 18874372
  133.0 4.1 %copy-start.2 = (f32[2,128]{1,0:T(2,128)S(1)}, f32[2,128]{1,0:T(2,128)}, u32[]{:S(2)}) copy-start(f32[2,128]{1,0:T(2,128)} %get-tuple-element.10) | copy-start | bytes 3076

commit v6 on v5

--- a/solution.py
+++ b/solution.py
@@ -410,6 +410,7 @@
 
     ones = jnp.ones((8, 128), BF16)
     last = (((1,), (1,)), ((), ()))
+    slices = []
     folds = [jnp.zeros((tokens, 128), F32), jnp.zeros((tokens, 128), F32)]
     for j in range(4):
         cols = slice(j * q_w, (j + 1) * q_w)
@@ -422,7 +423,7 @@
             terms = part * slot_out
             for k in range(q_w // 128):
                 folds[t] = folds[t] + terms[:, k * 128 : (k + 1) * 128]
-        mixed[j] = total.astype(BF16)
+        slices.append(total)
     for t in range(2):
         high = folds[t].astype(BF16)
         low = (folds[t] - high.astype(F32)).astype(BF16)
@@ -439,6 +440,7 @@
 
     for o in range(1, 4):
         cg_copy(o).start()
+    mixed[...] = jnp.stack(slices, axis=1).astype(BF16)
 
     pltpu.make_async_copy(bh, bh, home_recv.at[1]).wait()
 
@@ -489,7 +491,7 @@
     return pl.pallas_call(
         exchange_kernel,
         out_shape=(
-            jax.ShapeDtypeStruct((4, tokens, width // 4), BF16),
+            jax.ShapeDtypeStruct((tokens, 4, width // 4), BF16),
             jax.ShapeDtypeStruct((2, tokens, ff), F32),
             jax.ShapeDtypeStruct((ff, width), BF16),
             jax.ShapeDtypeStruct((2, tokens), F32),
@@ -547,7 +549,6 @@
     mixed, hg, wg, cg = exchange(
         slot_row, jnp.transpose(hidden, (1, 0, 2)), combine.T, out_grad, down_weight[0]
     )
-    mixed = jnp.transpose(mixed, (1, 0, 2))
     combine_grad = cg.T
     hidden_grad = jnp.transpose(hg, (1, 0, 2))
     gate_grad = (hidden_grad * up_f * sig * (1.0 + gate_f * (1.0 - sig))).astype(BF16)

time: 141 us -> 140 us (level)
    unnamed x11 -> x13, local copies, waits for them, and re-layouts: 9.42 us -> 8.12 us
where the time goes in v6:
time: 140 us
  Pallas kernels  123 us (88%)
  local copies, waits for them, and re-layouts  8.88 us (6%)
  other arithmetic  7.42 us (5%)
    pallas_call x1, Pallas kernels, exchange(): pl.pallas_call(exchange_kernel, out_shape=(jax.ShapeDtypeStruct((tokens,...  123 us
    unnamed x13, local copies, waits for them, and re-layouts  8.12 us
    transpose x1, other arithmetic, per_device(): jnp.transpose(hidden, (1, 0, 2))  3.52 us
    convert_element_type x1, other arithmetic, per_device(): up_grad = (hidden_grad * gate_f * sig).astype(BF16)  3.31 us

profile of v6, /device:TPU:1, one launch (start us, length us, event | category | flops | bytes accessed | tf_op | source)
XLA Modules:
  0.0 139.8 jit_solution(14946863139121563783)
XLA Ops:
  0.6 0.8 slice_bitcast_fusion.3
  1.4 0.2 fusion.10
  1.6 0.6 fusion.14.slot_row
  2.2 3.5 %fusion.11.hidden = bf16[2,128,2048]{2,1,0:T(8,128)(2,1)} fusion(bf16[128,2,2048]{2,1,0:T(2,128)(2,1)} %param.7, bf16[128,2,2048]{2,1,0:T(2,128)(2,1)} %param.6), kind=kLoop, calls=%fused_computation.18 | loop fusion | flops 4194304 | bytes 3145728 | tf_op jit(solution)/shard_map/transpose | solution.py:550
  5.7 0.0 copy-start.1
  5.7 122.6 %shard_map.101 = (bf16[128,4,384]{2,1,0:T(4,128)(2,1)}, f32[2,128,2048]{2,1,0:T(8,128)}, bf16[2048,1536]{1,0:T(8,128)(2,1)}, f32[2,128]{1,0:T(2,128)}) custom-call(s32[1,256]{1,0:T(1,128)} %fusion.14.slot_row, bf16[2,128,2048]{2,1,0:T(8,128)(2,1)} %fusion.11.hidden, f32[2,128]{1,0:T(2,128)} %bitcast.22, bf16[128,6144]{1,0:T(8,128)(2,1)} %grad_hbm.1, ...), custom_call_target="tpu_custom_call" | custom-call | flops 28991029248 | bytes 30000000 | tf_op jit(solution)/shard_map/pallas_call | solution.py:491
  128.3 0.0 copy-done.1
  128.3 0.0 copy-start
  128.3 3.3 %fusion.9 = (bf16[128,2,2048]{2,0,1:T(8,128)(2,1)S(1)}, bf16[128,2,2048]{2,0,1:T(8,128)(2,1)S(1)}) fusion(f32[2,128,2048]{2,1,0:T(8,128)} %get-tuple-element.11, bf16[128,2,2048]{2,1,0:T(2,128)(2,1)} %param.6, bf16[128,2,2048]{2,1,0:T(2,128)(2,1)S(1)} %copy-done.1), kind=kLoop, calls=%fused_computation.15 | loop fusion | flops 7864320 | bytes 6291456 | tf_op jit(solution)/shard_map/convert_element_type | solution.py:555
  131.6 0.0 copy-start.2
  131.6 0.0 copy-start.3
  131.6 2.0 %copy.14 = bf16[128,2,2048]{2,1,0:T(2,128)(2,1)} copy(bf16[128,2,2048]{2,0,1:T(8,128)(2,1)S(1)} %get-tuple-element.18) | data formatting | bytes 2097152
  133.7 2.0 %copy.13 = bf16[128,2,2048]{2,1,0:T(2,128)(2,1)} copy(bf16[128,2,2048]{2,0,1:T(8,128)(2,1)S(1)} %get-tuple-element.19) | data formatting | bytes 2097152
  135.7 0.0 copy-done.2
  135.7 0.7 copy.23
  136.5 0.0 copy-done.3
  136.5 0.6 copy.24
  137.1 0.0 copy-done
  137.1 2.7 %copy.25 = bf16[1,2048,1536]{2,1,0:T(8,128)(2,1)} copy(bf16[1,2048,1536]{2,1,0:T(8,128)(2,1)S(1)} %bitcast.18) | data formatting | bytes 12582912
  (2 shorter events, 0.0 us)
Async XLA Ops:
  5.7 122.6 %copy-start.1 = (bf16[128,2,2048]{2,1,0:T(2,128)(2,1)S(1)}, bf16[128,2,2048]{2,1,0:T(2,128)(2,1)}, u32[]{:S(2)}) copy-start(bf16[128,2,2048]{2,1,0:T(2,128)(2,1)} %param.7) | copy-start | bytes 3145732
  128.3 8.8 %copy-start = (bf16[2048,1536]{1,0:T(8,128)(2,1)S(1)}, bf16[2048,1536]{1,0:T(8,128)(2,1)}, u32[]{:S(2)}) copy-start(bf16[2048,1536]{1,0:T(8,128)(2,1)} %get-tuple-element.12) | copy-start | bytes 18874372
  131.6 4.1 %copy-start.2 = (bf16[128,4,384]{2,1,0:T(4,128)(2,1)S(1)}, bf16[128,4,384]{2,1,0:T(4,128)(2,1)}, u32[]{:S(2)}) copy-start(bf16[128,4,384]{2,1,0:T(4,128)(2,1)} %get-tuple-element.29) | copy-start | bytes 1179652
  131.6 4.9 %copy-start.3 = (f32[2,128]{1,0:T(2,128)S(1)}, f32[2,128]{1,0:T(2,128)}, u32[]{:S(2)}) copy-start(f32[2,128]{1,0:T(2,128)} %get-tuple-element.10) | copy-start | bytes 3076
